TPU v7x, 32 devices: a whole 2x2x4 slice. The times are simulated.
32 devices in a mesh: group: 2 (over x), replica: 16 (over z, y, core).
Axes of the slice: x: 2, y: 2, z: 4, core: 2. Of those that a mesh axis runs over, the one named last changes fastest.
Arguments:
- hidden_in: bfloat16 [10240, 3072], P(('group', 'replica')), may hold values from -8 to 8
- w_query: bfloat16 [3072, 1536], replicated, may hold values from -0.109375 to 0.109375
- query_gain: float32 [128], replicated, may hold values from 0.5 to 2
- down_projection_matrix: bfloat16 [3072, 64], replicated, may hold values from -0.23925781 to 0.23925781
- up_projection_matrix: bfloat16 [64, 1536], replicated, may hold values from -0.59765625 to 0.59765625
- query_cotangent: bfloat16 [10240, 1536], P(('group', 'replica')), may hold values from -8 to 8
- first_moment: float32 [4608, 64], P(('group', 'replica')), may hold values from -3 to 3
- second_moment: float32 [4608, 64], P(('group', 'replica')), may hold values from 0.001 to 0.1
Outputs:
- new_down: bfloat16 [3072, 64], replicated
- new_up: bfloat16 [64, 1536], replicated
- first_next: float32 [4608, 64], P(('group', 'replica'))
- second_next: float32 [4608, 64], P(('group', 'replica'))
All inputs are finite; a program needn't handle non-finite values.
Results may differ from a plain program's by a relative error of at most 0.0019.
Values may be sent and summed in bfloat16 or wider, within the bound.
No kernel may reach another device: no remote copies, remote signals or barrier semaphores. Data moves between devices by JAX's collectives and lax.ppermute only.
A program may use at most 64 MiB of HBM per device.

v0:
```python
import jax
import jax.numpy as jnp
from jax import lax
from jax.sharding import PartitionSpec as P

adapter_scale_factor = 0.5
norm_epsilon = 1e-06
beta_one = 0.9
beta_two = 0.999
first_bias = 1.0 - 0.9**10
second_bias = 1.0 - 0.999**10
learn_rate = 0.001
adam_eps = 1e-08


def queries_backward(
    rows_in, grads_in, w_query, query_gain, down_projection_matrix, up_projection_matrix
):
    reduced_rank_input = jnp.dot(
        rows_in, down_projection_matrix, preferred_element_type=jnp.float32
    ).astype(jnp.bfloat16)
    apply_projection = jnp.dot(rows_in, w_query, preferred_element_type=jnp.float32)
    apply_projection = apply_projection + adapter_scale_factor * jnp.dot(
        reduced_rank_input, up_projection_matrix, preferred_element_type=jnp.float32
    )
    token_count = apply_projection.shape[0]
    head_size = query_gain.shape[0]
    shaped = apply_projection.reshape(token_count, -1, head_size)
    inverse = lax.rsqrt(jnp.mean(shaped * shaped, axis=-1, keepdims=True) + norm_epsilon)
    normed = shaped * inverse
    upstream = grads_in.astype(jnp.float32).reshape(shaped.shape) * query_gain
    grad_pre = inverse * (upstream - normed * jnp.mean(upstream * normed, axis=-1, keepdims=True))
    grad_pre = grad_pre.reshape(token_count, -1).astype(jnp.bfloat16)
    backward_reduced = lax.dot_general(
        grad_pre, up_projection_matrix, (((1,), (1,)), ((), ())), preferred_element_type=jnp.float32
    )
    backward_reduced = (adapter_scale_factor * backward_reduced).astype(jnp.bfloat16)
    scaled_reduced = (reduced_rank_input.astype(jnp.float32) * adapter_scale_factor).astype(
        jnp.bfloat16
    )
    return (grad_pre, backward_reduced, scaled_reduced)


def adam_update(grads, params, first, second):
    first_new = beta_one * first + (1.0 - beta_one) * grads
    second_new = beta_two * second + (1.0 - beta_two) * grads * grads
    direction = first_new / first_bias / (jnp.sqrt(second_new / second_bias) + adam_eps)
    return ((params - learn_rate * direction).astype(jnp.bfloat16), first_new, second_new)


def on_device(
    hidden_in,
    w_query,
    query_gain,
    down_projection_matrix,
    up_projection_matrix,
    query_cotangent,
    first_moment,
    second_moment,
):
    model_width = hidden_in.shape[1]
    adapter_rank_size = down_projection_matrix.shape[1]
    row_count_total = model_width + up_projection_matrix.shape[1]
    accelerator_list = lax.axis_size("group") * lax.axis_size("replica")
    own_rows = row_count_total // accelerator_list
    grad_pre, backward_reduced, scaled_reduced = queries_backward(
        hidden_in,
        query_cotangent,
        w_query,
        query_gain,
        down_projection_matrix,
        up_projection_matrix,
    )
    stacked = jnp.concatenate([hidden_in, grad_pre], axis=1)
    operand = jnp.concatenate([backward_reduced, scaled_reduced], axis=1)
    matrix_product = lax.dot_general(
        stacked, operand, (((0,), (0,)), ((), ())), preferred_element_type=jnp.float32
    )
    row_ids = lax.iota(jnp.int32, lax.axis_size(("group", "replica")) * own_rows)
    is_down_matrix = (row_ids < model_width)[:, None]
    grad_own = lax.psum_scatter(
        jnp.where(
            is_down_matrix,
            matrix_product[:, :adapter_rank_size],
            matrix_product[:, adapter_rank_size:],
        )
        / accelerator_list,
        ("group", "replica"),
        scatter_dimension=0,
        tiled=True,
    )
    owner = lax.axis_index(("group", "replica"))
    combined = jnp.concatenate([down_projection_matrix, up_projection_matrix.T], axis=0)
    params_own = lax.dynamic_slice_in_dim(combined, owner * own_rows, own_rows, 0).astype(
        jnp.float32
    )
    updated_own, first_new, second_new = adam_update(
        grad_own, params_own, first_moment, second_moment
    )
    gathered = lax.all_gather(updated_own, ("group", "replica"), axis=0, tiled=True)
    return (gathered[:model_width], gathered[model_width:].T, first_new, second_new)


def solution(mesh):
    placed = (
        P(("group", "replica"), None),
        P(),
        P(),
        P(),
        P(),
        P(("group", "replica"), None),
        P(("group", "replica"), None),
        P(("group", "replica"), None),
    )
    return jax.shard_map(
        on_device,
        mesh=mesh,
        in_specs=placed,
        out_specs=(P(), P(), P(("group", "replica"), None), P(("group", "replica"), None)),
        check_vma=False,
    )
```

profile of v0, /device:TPU:0, one launch (start us, length us, event | category | flops | bytes accessed | tf_op | source)
XLA Modules:
  0.0 195.9 jit_solution(10893317597869089222)
XLA Ops:
  7.2 0.0 copy-start.1
  7.2 0.0 reduce-scatter.4.cloned.1.call-start
  7.2 3.1 %multiply_convert_fusion.1 = (bf16[320,64]{0,1:T(8,128)(2,1)}, bf16[320,64]{0,1:T(8,128)(2,1)S(1)}) fusion(bf16[320,3072]{1,0:T(8,128)(2,1)} %param.8, bf16[3072,64]{0,1:T(8,128)(2,1)} %param.11), kind=kOutput, calls=%fused_computation.21 | convolution fusion | flops 125911040 | bytes 2441216 | tf_op jit(solution)/shard_map/dot_general | solution.py:19
  10.3 0.0 copy-done.1
  10.3 5.8 %fusion.15 = f32[320,1536]{1,0:T(8,128)S(1)} fusion(bf16[320,3072]{1,0:T(8,128)(2,1)S(1)} %copy-done.1, bf16[3072,1536]{1,0:T(8,128)(2,1)} %param.9), kind=kOutput, calls=%fused_computation.32 | convolution fusion | flops 3019898880 | bytes 13369344 | tf_op jit(solution)/shard_map/dot_general | solution.py:22
  16.1 1.7 fusion.4
  17.8 2.0 %copy.18 = f32[320,1536]{0,1:T(8,128)S(1)} copy(f32[320,1536]{1,0:T(8,128)} %fusion.4) | data formatting | bytes 3932160 | tf_op jit(solution)/shard_map/add | solution.py:23
  19.8 0.0 copy-start.3
  19.8 0.2 multiply_reduce_fusion.1
  20.0 0.6 add_rsqrt_fusion
  20.6 0.4 copy-done.3
  21.0 1.7 copy.20
  22.7 0.7 broadcast_bitcast_fusion
  23.4 2.2 %multiply_reduce_fusion = f32[320,12]{0,1:T(8,128)S(1)} fusion(f32[320,12,128]{0,2,1:T(8,128)S(1)} %bitcast.23, f32[320,12,128]{0,2,1:T(8,128)} %bitcast.24, f32[128]{0:T(128)} %param.10, f32[320,12]{0,1:T(8,128)} %add_rsqrt_fusion), kind=kLoop, calls=%fused_computation.6 | loop fusion | flops 1962240 | bytes 3963392 | tf_op jit(solution)/shard_map/reduce_sum | solution.py:32
  25.6 0.2 mul.117
  25.7 1.9 copy.21
  27.6 2.3 %mul.106 = f32[320,12,128]{0,2,1:T(8,128)} broadcast(f32[320,12]{0,1:T(8,128)} %add_rsqrt_fusion), dimensions={0,1} | broadcast | bytes 1981440 | tf_op jit(solution)/shard_map/mul | solution.py:32
  29.9 3.1 %copy.22 = f32[320,1536]{1,0:T(8,128)} copy(f32[320,1536]{0,1:T(8,128)} %bitcast.26) | data formatting | bytes 3932160 | tf_op jit(solution)/shard_map/mul | solution.py:32
  33.1 3.0 %multiply_convert_fusion = bf16[320,1536]{1,0:T(8,128)(2,1)S(1)} fusion(f32[320,1536]{1,0:T(8,128)} %copy.22, f32[320,1536]{1,0:T(8,128)} %copy.21, f32[320,1536]{1,0:T(8,128)S(1)} %copy-done, f32[1536]{0:T(1024)S(1)} %broadcast_bitcast_fusion, bf16[320,1536]{1,0:T(8,128)(2,1)S(1)} %copy-done.3), kind=kLoop, calls=%fused_computation.8 | loop fusion | flops 3440640 | bytes 7870464 | tf_op jit(solution)/shard_map/convert_element_type | solution.py:33
  36.1 0.4 fusion.6
  36.5 0.8 fusion
  37.3 0.1 fusion.5
  37.5 1.9 copy.24
  39.4 0.0 reduce-scatter.4.cloned.1.call-update
  39.4 101.9 %reduce-scatter.4.cloned.1.call-done = f32[144,64]{1,0:T(8,128)} async-done(((f32[4608,64]{1,0:T(8,128)}), f32[144,64]{1,0:T(8,128)}) %reduce-scatter.4.cloned.1.call-update) | async-done | bytes 36880
  141.3 1.0 copy.25
  142.3 0.7 fusion.12
  143.0 42.3 %all-gather = bf16[32,144,64]{1,2,0:T(8,128)(2,1)S(1)} all-gather(bf16[1,144,64]{1,2,0:T(8,128)(2,1)S(1)} %get-tuple-element.4), channel_id=1, replica_groups=mesh['group'=2,'replica'=16] {'group','replica'}, dimensions={0}, use_global_device_ids=true | all-gather | bytes 608256 | tf_op jit(solution)/shard_map/all_gather | solution.py:100
  185.3 0.6 copy.23
  185.9 1.7 reshape.39
  187.6 0.8 slice.18
  188.4 0.7 slice_bitcast_fusion
  (16 shorter events, 0.0 us)
Async XLA Ops:
  7.2 3.1 %copy-start.1 = (bf16[320,3072]{1,0:T(8,128)(2,1)S(1)}, bf16[320,3072]{1,0:T(8,128)(2,1)}, u32[]{:S(2)}) copy-start(bf16[320,3072]{1,0:T(8,128)(2,1)} %param.8) | copy-start | bytes 5898244
  7.2 134.1 %reduce-scatter.4.cloned.1.call-start = ((), (), s32[]{:S(2)}) async-start(), calls=%async_computation.1 | async-start | bytes 2433024
  10.3 5.8 %copy-start.4 = (bf16[64,1536]{1,0:T(8,128)(2,1)S(1)}, bf16[64,1536]{1,0:T(8,128)(2,1)}, u32[]{:S(2)}) copy-start(bf16[64,1536]{1,0:T(8,128)(2,1)} %param.12) | copy-start | bytes 589828
  19.8 1.2 copy-start.3
  29.9 3.1 %copy-start = (f32[320,1536]{1,0:T(8,128)S(1)}, f32[320,1536]{1,0:T(8,128)}, u32[]{:S(2)}) copy-start(f32[320,1536]{1,0:T(8,128)} %fusion.4) | copy-start | bytes 5898244
  33.1 3.5 %copy-start.2 = (bf16[320,3072]{1,0:T(8,128)(2,1)S(1)}, bf16[320,3072]{1,0:T(8,128)(2,1)}, u32[]{:S(2)}) copy-start(bf16[320,3072]{1,0:T(8,128)(2,1)} %param.8) | copy-start | bytes 5898244
  33.1 3.5 %copy-start.6 = (bf16[320,64]{0,1:T(8,128)(2,1)S(1)}, bf16[320,64]{0,1:T(8,128)(2,1)}, u32[]{:S(2)}) copy-start(bf16[320,64]{0,1:T(8,128)(2,1)} %get-tuple-element.7) | copy-start | bytes 122884
  39.4 102.9 %copy-start.5 = (bf16[3072,64]{0,1:T(8,128)(2,1)S(1)}, bf16[3072,64]{0,1:T(8,128)(2,1)}, u32[]{:S(2)}) copy-start(bf16[3072,64]{0,1:T(8,128)(2,1)} %param.11) | copy-start | bytes 1179652
  39.4 102.9 %copy-start.7 = (f32[144,64]{0,1:T(8,128)S(1)}, f32[144,64]{0,1:T(8,128)}, u32[]{:S(2)}) copy-start(f32[144,64]{0,1:T(8,128)} %param.14) | copy-start | bytes 110596
  39.4 102.9 %copy-start.8 = (f32[144,64]{0,1:T(8,128)S(1)}, f32[144,64]{0,1:T(8,128)}, u32[]{:S(2)}) copy-start(f32[144,64]{0,1:T(8,128)} %param.15) | copy-start | bytes 110596
Sparse Core Ops, SparseCore 0:
  39.5 101.7 reduce-scatter.3
where the time goes:
time: 196 us
  waiting for transfers between devices  102 us (52%)
  blocking collectives  42.3 us (22%)
  local copies, waits for them, and re-layouts  18.8 us (10%)
  between operations  14.2 us (7%)
  matrix products  11.8 us (6%)
  other arithmetic  6.9 us (4%)
    unnamed x2, waiting for transfers between devices  102 us
    all_gather x1, blocking collectives, on_device(): lax.all_gather(updated_own, ('group', 'replica'), axis=0, tiled=True)  42.3 us
    dot_general x1, matrix products, queries_backward(): jnp.dot(rows_in, w_query, preferred_element_type=jnp.float32)  5.78 us
    mul x2, local copies, waits for them, and re-layouts, queries_backward(): inverse * (upstream - normed * jnp.mean(upstream * normed, axis=-1, keepd...  5.43 us
    unnamed x21, local copies, waits for them, and re-layouts  4.92 us
  transfers between devices with their start and end apart: 1, of which 1 were waited for; matrix products, arithmetic and copies ran while one was open for 0% of the time, Pallas kernels for 0%

commit v1 on v0

v1 whole, which is shorter than its diff:
```python
import functools

import jax
import jax.numpy as jnp
from jax import lax
from jax.experimental import pallas as pl
from jax.experimental.pallas import tpu as pltpu
from jax.sharding import Mesh
from jax.sharding import PartitionSpec as P

adapter_scale_factor = 0.5
norm_epsilon = 1e-06
beta_one = 0.9
beta_two = 0.999
first_bias = 1.0 - 0.9**10
second_bias = 1.0 - 0.999**10
learn_rate = 0.001
adam_eps = 1e-08

LANES = 128
SUB = 8
EXTRA = 8
TOP = 14.0
TINY = 1e-30
F32 = jnp.float32
BF16 = jnp.bfloat16
EVERY = ("group", "chip", "core")
CHIPS = ("group", "chip")
SWAP = ((0, 1), (1, 0))


def lanes_of(shape):
    return lax.broadcasted_iota(jnp.int32, shape, len(shape) - 1)


def pack_tail(tile, start):
    step = LANES // SUB
    group = lanes_of((SUB, LANES)) // step
    out = None
    for r in range(SUB):
        part = tile[SUB * r : SUB * (r + 1), :]
        shift = (step * r - start) % LANES
        if not isinstance(shift, int) or shift:
            part = pltpu.roll(part, shift, 1)
        out = part if out is None else jnp.where(group == r, part, out)
    return out


def unpack_tail(tail, start):
    step = LANES // SUB
    parts = []
    for r in range(SUB):
        shift = (start - step * r) % LANES
        moved = not isinstance(shift, int) or shift
        parts.append(pltpu.roll(tail, shift, 1) if moved else tail)
    return jnp.concatenate(parts, axis=0)


def backward_kernel(
    steps,
    where_ref,
    hidden_ref,
    w_ref,
    gain_ref,
    down_ref,
    up_ref,
    cot_ref,
    *rest,
    packed,
):
    if packed:
        (first_ref, second_ref, keep_ref, send_ref, own_ref, scaled_s, back_s, grads_s, params_s) = rest
    else:
        grads_s, scaled_s, back_s = rest
    step = pl.program_id(0)
    width = w_ref.shape[1]
    head = gain_ref.shape[1]
    model_width = hidden_ref.shape[1]

    @pl.when(step == 0)
    def _():
        low = lax.dot_general(
            hidden_ref[...], down_ref[...], (((1,), (1,)), ((), ())), preferred_element_type=F32
        ).astype(BF16)
        scaled_s[...] = (low.astype(F32) * adapter_scale_factor).astype(BF16)
        back_s[...] = jnp.zeros_like(back_s)
        if packed:
            params_s[:, :model_width] = down_ref[...]

    scaled = scaled_s[...]
    up = up_ref[...]
    project = jnp.dot(hidden_ref[...], w_ref[...], preferred_element_type=F32)
    project = project + jnp.dot(scaled, up, preferred_element_type=F32)
    pieces = []
    for h in range(width // head):
        mine = project[:, h * head : (h + 1) * head]
        inverse = lax.rsqrt(jnp.mean(mine * mine, axis=-1, keepdims=True) + norm_epsilon)
        normed = mine * inverse
        upstream = cot_ref[:, h * head : (h + 1) * head].astype(F32) * gain_ref[...]
        mean = jnp.mean(upstream * normed, axis=-1, keepdims=True)
        pieces.append((inverse * (upstream - normed * mean)).astype(BF16))
    grad_pre = jnp.concatenate(pieces, axis=1)
    back_s[...] += lax.dot_general(
        grad_pre, up, (((1,), (1,)), ((), ())), preferred_element_type=F32
    )
    place = pl.ds(pl.multiple_of(model_width + step * width, LANES), width)
    grads_s[:, place] = lax.dot_general(
        scaled, grad_pre, (((0,), (0,)), ((), ())), preferred_element_type=F32
    )
    if packed:
        params_s[:, place] = up

    @pl.when(step == steps - 1)
    def _():
        back_low = (adapter_scale_factor * back_s[...]).astype(BF16)
        grads_s[:, :model_width] = lax.dot_general(
            back_low, hidden_ref[...], (((0,), (0,)), ((), ())), preferred_element_type=F32
        )
        if packed:
            pack_blocks(where_ref, grads_s, params_s, first_ref, second_ref, keep_ref, send_ref, own_ref)


def pack_blocks(where_ref, grads_s, params_s, first_ref, second_ref, keep_ref, send_ref, own_ref):
    lane = lanes_of((64, LANES))
    core = where_ref[1]
    on_zero = jnp.full((SUB, LANES), core, jnp.int32) == 0
    on_zero_main = jnp.full((64, LANES), core, jnp.int32) == 0

    def block_of(i):
        j, tile = i % SUB, i // SUB * (SUB + 1) + i % SUB
        a = grads_s[:, tile * LANES : (tile + 1) * LANES]
        b = grads_s[:, (tile + 1) * LANES : (tile + 2) * LANES]
        main = jnp.where(lane >= 16 * j, a, b) if j else a
        tail = pack_tail(b, 16 * j)
        top = jnp.maximum(jnp.max(jnp.abs(main)), jnp.max(jnp.abs(tail)))
        return main, tail, jnp.full((SUB, LANES), top, F32)

    for k in range(keep_ref.shape[0]):
        even, odd = block_of(2 * k), block_of(2 * k + 1)
        for ref, (one, two) in ((keep_ref, (even, odd)), (send_ref, (odd, even))):
            ref[k, :64] = jnp.where(on_zero_main, one[0], two[0])
            ref[k, 64:72] = jnp.where(on_zero, one[1], two[1])
            ref[k, 72:80] = jnp.where(on_zero, one[2], two[2])

    index = where_ref[0]
    j = index % SUB
    tile = index // SUB * (SUB + 1) + j
    window = params_s[:, pl.ds(pl.multiple_of(tile * LANES, LANES), 2 * LANES)].astype(F32)
    a, b = window[:, :LANES], window[:, LANES:]
    own_ref[0, :64] = jnp.where(lane >= 16 * j, a, b)
    own_ref[0, 64:72] = pack_tail(b, 16 * j)
    for n, ref in ((1, first_ref), (2, second_ref)):
        own_ref[n, :64] = pltpu.roll(ref[:, :LANES], 16 * j, 1)
        last = jnp.concatenate([ref[:, LANES:], jnp.zeros((64, LANES - 16), F32)], axis=1)
        own_ref[n, 64:72] = pack_tail(last, 0)


def finish_kernel(where_ref, mine_ref, other_ref, own_ref, down_ref, up_ref, first_ref, second_ref):
    lane = lanes_of((64, LANES))
    core = where_ref[1]
    on_zero = jnp.full((80, LANES), core, jnp.int32) == 0
    down_tiles = down_ref.shape[1] // LANES
    blocks = {}

    def block_of(i):
        if i not in blocks:
            blocks.clear()
            k = i // 2
            one, two = mine_ref[k].astype(F32), other_ref[k].astype(F32)
            blocks[2 * k] = jnp.where(on_zero, one, two)
            blocks[2 * k + 1] = jnp.where(on_zero, two, one)
        return blocks[i]

    tiles = (down_ref.shape[1] + up_ref.shape[1]) // LANES
    before = None
    for tile in range(tiles):
        group, t = tile // (SUB + 1), tile % (SUB + 1)
        value = None
        if t < SUB:
            value = block_of(SUB * group + t)
        out = value[:64] if t == 0 else None
        if t:
            out = unpack_tail(before[64:72], 16 * (t - 1))
            if t > 1:
                out = jnp.where(lane < 16 * (t - 1), before[:64], out)
            if t < SUB:
                out = jnp.where(lane >= 16 * t, value[:64], out)
        before = value
        out = out.astype(BF16)
        if tile < down_tiles:
            down_ref[:, tile * LANES : (tile + 1) * LANES] = out
        else:
            up_ref[:, (tile - down_tiles) * LANES : (tile - down_tiles + 1) * LANES] = out

    j = where_ref[0] % SUB
    for n, ref in ((0, first_ref), (1, second_ref)):
        ref[:, :LANES] = pltpu.roll(own_ref[n, :64], (LANES - 16 * j) % LANES, 1)
        ref[:, LANES:] = unpack_tail(own_ref[n, 64:72], 0)[:, :16]


def whole(shape):
    return pl.BlockSpec(shape, lambda s: (0,) * len(shape), pipeline_mode=pl.Buffered(1))


def backward(where, hidden, w_query, gain, down_t, up, cotangent, first_t, second_t, chips, packed):
    tokens, model_width = hidden.shape
    features = w_query.shape[1]
    rank = down_t.shape[0]
    head = gain.shape[1]
    width = 2 * head if features % (2 * head) == 0 else head
    steps = features // width
    rows = model_width + features
    columns = lambda n: pl.BlockSpec((n, width), lambda s: (0, s))
    in_specs = [
        pl.BlockSpec(memory_space=pltpu.SMEM),
        whole((tokens, model_width)),
        columns(model_width),
        whole((1, head)),
        whole((rank, model_width)),
        columns(rank),
        columns(tokens),
    ]
    operands = [where, hidden, w_query, gain, down_t, up, cotangent]
    scratch = [pltpu.VMEM((tokens, rank), BF16), pltpu.VMEM((tokens, rank), F32)]
    if packed:
        own = rows // chips // 2
        height = rank * own // LANES
        halves = (chips, height + EXTRA, LANES)
        in_specs += [whole((rank, own))] * 2
        operands += [first_t, second_t]
        out_shape = [jax.ShapeDtypeStruct(halves, F32)] * 2 + [
            jax.ShapeDtypeStruct((3, height, LANES), F32)
        ]
        out_specs = [whole(halves)] * 2 + [whole((3, height, LANES))]
        scratch += [pltpu.VMEM((rank, rows), F32), pltpu.VMEM((rank, rows), BF16)]
    else:
        out_shape = jax.ShapeDtypeStruct((rank, rows), F32)
        out_specs = whole((rank, rows))
    return pl.pallas_call(
        functools.partial(backward_kernel, steps, packed=packed),
        grid=(steps,),
        in_specs=in_specs,
        out_specs=out_specs,
        out_shape=out_shape,
        scratch_shapes=scratch,
        compiler_params=pltpu.CompilerParams(
            dimension_semantics=("arbitrary",), vmem_limit_bytes=48 << 20
        ),
        name="backward",
    )(*operands)


def finish(where, mine, other, own_new, model_width, features):
    rank = 64
    own = own_new.shape[1] * LANES // rank
    full = pl.BlockSpec(memory_space=pltpu.VMEM)
    return pl.pallas_call(
        finish_kernel,
        in_specs=[pl.BlockSpec(memory_space=pltpu.SMEM), full, full, full],
        out_specs=[full] * 4,
        out_shape=[
            jax.ShapeDtypeStruct((rank, model_width), BF16),
            jax.ShapeDtypeStruct((rank, features), BF16),
            jax.ShapeDtypeStruct((rank, own), F32),
            jax.ShapeDtypeStruct((rank, own), F32),
        ],
        compiler_params=pltpu.CompilerParams(vmem_limit_bytes=32 << 20),
        name="finish",
    )(where, mine, other, own_new)


def rows_of(columns):
    return columns.reshape(-1, LANES)


def on_device(
    hidden_in,
    w_query,
    query_gain,
    down_projection_matrix,
    up_projection_matrix,
    query_cotangent,
    first_moment,
    second_moment,
):
    model_width, rank = down_projection_matrix.shape
    features = up_projection_matrix.shape[1]
    chips = lax.axis_size(CHIPS)
    devices = 2 * chips
    own = (model_width + features) // devices
    height = rank * own // LANES
    packed = rank == 64 and own == LANES + 16 and model_width % LANES == 0 and chips % 4 == 0
    core = lax.axis_index("core")
    index = lax.axis_index(EVERY)
    where = jnp.stack([index, core]).astype(jnp.int32)
    down_t = down_projection_matrix.T
    result = backward(
        where,
        hidden_in,
        w_query,
        query_gain[None, :],
        down_t,
        up_projection_matrix,
        query_cotangent,
        first_moment.T,
        second_moment.T,
        chips,
        packed,
    )
    if packed:
        keep, send, own_state = result
        params, first, second = own_state[0], own_state[1], own_state[2]
    else:
        blocks = result.reshape(rank, chips, 2, own).transpose(2, 1, 0, 3).reshape(2, chips, height, LANES)
        top = jnp.max(jnp.abs(blocks), axis=(2, 3), keepdims=True)
        blocks = jnp.concatenate([blocks, jnp.broadcast_to(top, (2, chips, EXTRA, LANES))], axis=2)
        keep = lax.dynamic_index_in_dim(blocks, core, 0, keepdims=False)
        send = lax.dynamic_index_in_dim(blocks, 1 - core, 0, keepdims=False)
        combined = jnp.concatenate([down_t, up_projection_matrix], axis=1)
        params = rows_of(lax.dynamic_slice_in_dim(combined, index * own, own, 1)).astype(F32)
        first, second = rows_of(first_moment.T), rows_of(second_moment.T)

    other = lax.ppermute(send, "core", SWAP)
    total = keep + other
    bound = jnp.maximum(keep[:, height : height + 1] + other[:, height : height + 1], TINY)
    power = jnp.ceil(jnp.log2(bound)) - TOP
    is_value = lax.broadcasted_iota(jnp.int32, total.shape, 1) < height
    coded = jnp.where(is_value, total * jnp.exp2(-power), power).astype(jnp.float16)
    arrived = lax.all_to_all(coded, CHIPS, 0, 0, tiled=True)

    grads = None
    for k in range(chips):
        power = arrived[k, height : height + 1].astype(F32)
        term = arrived[k, :height].astype(F32) * jnp.exp2(power)
        grads = term if grads is None else grads + term
    grads = grads / devices
    first_new = beta_one * first + (1.0 - beta_one) * grads
    second_new = beta_two * second + (1.0 - beta_two) * grads * grads
    direction = first_new / first_bias / (jnp.sqrt(second_new / second_bias) + adam_eps)
    updated = (params - learn_rate * direction).astype(BF16)

    updated = jnp.pad(updated, ((0, EXTRA), (0, 0)))
    copies = jnp.broadcast_to(updated[None], (chips, height + EXTRA, LANES))
    mine = lax.all_to_all(copies, CHIPS, 0, 0, tiled=True)
    other = lax.ppermute(mine, "core", SWAP)
    if packed:
        own_new = jnp.stack([first_new, second_new])
        down_new, up_new, first_out, second_out = finish(where, mine, other, own_new, model_width, features)
    else:
        pair = jnp.stack([mine, other])
        pair = jnp.where(core == 0, pair, pair[::-1])[:, :, :height]
        columns = pair.reshape(2, chips, rank, own).transpose(2, 1, 0, 3).reshape(rank, devices * own)
        down_new, up_new = columns[:, :model_width], columns[:, model_width:]
        first_out, second_out = first_new.reshape(rank, own), second_new.reshape(rank, own)
    return (down_new.T, up_new, first_out.T, second_out.T)


def solution(mesh):
    groups, replicas = mesh.shape["group"], mesh.shape["replica"]
    fine = Mesh(mesh.devices.reshape(groups, replicas // 2, 2), EVERY)
    rows = P(EVERY, None)
    return jax.shard_map(
        on_device,
        mesh=fine,
        in_specs=(rows, P(), P(), P(), P(), rows, rows, rows),
        out_specs=(P(), P(), rows, rows),
        check_vma=False,
    )
```

time: 196 us -> 60.6 us (0.31)
  waiting for transfers between devices: 102 us -> 13.8 us
  blocking collectives: 42.3 us -> 19.7 us
  between operations: 14.2 us -> 0.7 us
  Pallas kernels: 0 us -> 13.4 us
  matrix products: 11.8 us -> 0 us
  local copies, waits for them, and re-layouts: 18.8 us -> 7.78 us
  other arithmetic: 6.9 us -> 0.52 us
  starting transfers between devices: 0.04 us -> 4.06 us
    unnamed x2 -> x0, waiting for transfers between devices: 102 us -> none
    all_gather x1 -> x0, blocking collectives: 42.3 us -> none  [on_device(): lax.all_gather(updated_own, ('group', 'replica'), axis=0, tiled=True)]
    all_to_all x0 -> x1, blocking collectives: none -> 19.7 us  [on_device(): arrived = lax.all_to_all(coded, CHIPS, 0, 0, tiled=True)]
    pallas_call x0 -> x2, Pallas kernels: none -> 13.4 us  [the longest x1 11.9 us: backward(): pl.pallas_call(functools.partial(backward_kernel, steps, packed=packed),...]
    dot_general x5 -> x0, matrix products: 11.8 us -> none  [the longest x1 5.78 us: queries_backward(): jnp.dot(rows_in, w_query, preferred_element_type=jnp.float32)]
    all_to_all x0 -> x1, waiting for transfers between devices: none -> 10.5 us  [on_device(): mine = lax.all_to_all(copies, CHIPS, 0, 0, tiled=True)]
    mul x5 -> x0, local copies, waits for them, and re-layouts: 8.11 us -> none  [the longest x2 5.43 us: queries_backward(): inverse * (upstream - normed * jnp.mean(upstream * normed, axis=-1, keepd...]
    all_to_all x0 -> x1, starting transfers between devices: none -> 3.54 us  [on_device(): mine = lax.all_to_all(copies, CHIPS, 0, 0, tiled=True)]
  transfers between devices with their start and end apart: 1 -> 3, of which waited for: 1 -> 3; matrix products, arithmetic and copies ran while one was open for 0% -> 0% of each run, Pallas kernels for 0% -> 0%
where the time goes in v1:
time: 60.6 us; the launch traced here: 60 us
  blocking collectives  19.7 us (33%)
  waiting for transfers between devices  13.8 us (23%)
  Pallas kernels  13.4 us (22%)
  local copies, waits for them, and re-layouts  7.78 us (13%)
  starting transfers between devices  4.06 us (7%)
  between operations  0.7 us (1%)
    all_to_all x1, blocking collectives, on_device(): arrived = lax.all_to_all(coded, CHIPS, 0, 0, tiled=True)  19.7 us
    pallas_call x1, Pallas kernels, backward(): pl.pallas_call(functools.partial(backward_kernel, steps, packed=packed),...  11.9 us
    all_to_all x1, waiting for transfers between devices, on_device(): mine = lax.all_to_all(copies, CHIPS, 0, 0, tiled=True)  10.5 us
    unnamed x14, local copies, waits for them, and re-layouts  7 us
    all_to_all x1, starting transfers between devices, on_device(): mine = lax.all_to_all(copies, CHIPS, 0, 0, tiled=True)  3.54 us
    ppermute x1, waiting for transfers between devices, on_device(): other = lax.ppermute(send, 'core', SWAP)  1.72 us
    ppermute x1, waiting for transfers between devices, on_device(): other = lax.ppermute(mine, 'core', SWAP)  1.6 us
    pallas_call x1, Pallas kernels, finish(): pl.pallas_call(finish_kernel, in_specs=[pl.BlockSpec(memory_space=pltpu.S...  1.56 us
  transfers between devices with their start and end apart: 3, of which 3 were waited for; matrix products, arithmetic and copies ran while one was open for 0% of the time, Pallas kernels for 0%

profile of v1, /device:TPU:0, one launch (start us, length us, event | category | flops | bytes accessed | tf_op | source)
XLA Modules:
  0.0 60.0 jit_solution(10704375296427456801)
XLA Ops:
  0.6 0.1 pad_add_fusion.where_ref
  0.7 0.0 copy-start
  0.7 1.5 %copy-done = bf16[320,3072]{1,0:T(8,128)(2,1)S(1)} copy-done((bf16[320,3072]{1,0:T(8,128)(2,1)S(1)}, bf16[320,3072]{1,0:T(8,128)(2,1)}, u32[]{:S(2)}) %copy-start) | copy-done | bytes 1966104
  2.3 0.0 copy-start.1
  2.3 1.2 %copy-done.1 = bf16[320,1536]{1,0:T(8,128)(2,1)S(1)} copy-done((bf16[320,1536]{1,0:T(8,128)(2,1)S(1)}, bf16[320,1536]{1,0:T(8,128)(2,1)}, u32[]{:S(2)}) %copy-start.1) | copy-done | bytes 983064
  3.5 0.0 copy-start.2
  3.5 1.0 %copy-done.2 = bf16[3072,64]{0,1:T(8,128)(2,1)S(1)} copy-done((bf16[3072,64]{0,1:T(8,128)(2,1)S(1)}, bf16[3072,64]{0,1:T(8,128)(2,1)}, u32[]{:S(2)}) %copy-start.2) | copy-done | bytes 393240
  4.5 0.0 copy-start.3
  4.5 0.9 %copy-done.3 = bf16[64,1536]{1,0:T(8,128)(2,1)S(1)} copy-done((bf16[64,1536]{1,0:T(8,128)(2,1)S(1)}, bf16[64,1536]{1,0:T(8,128)(2,1)}, u32[]{:S(2)}) %copy-start.3) | copy-done | bytes 196632
  5.4 0.0 copy-start.4
  5.4 0.8 %copy-done.4 = f32[144,64]{0,1:T(8,128)S(1)} copy-done((f32[144,64]{0,1:T(8,128)S(1)}, f32[144,64]{0,1:T(8,128)}, u32[]{:S(2)}) %copy-start.4) | copy-done | bytes 36888
  6.2 0.0 copy-start.5
  6.2 0.8 %copy-done.5 = f32[144,64]{0,1:T(8,128)S(1)} copy-done((f32[144,64]{0,1:T(8,128)S(1)}, f32[144,64]{0,1:T(8,128)}, u32[]{:S(2)}) %copy-start.5) | copy-done | bytes 36888
  7.1 0.0 copy-start.6
  7.1 0.7 %copy-done.6 = f32[128]{0:T(128)S(1)} copy-done((f32[128]{0:T(128)S(1)}, f32[128]{0:T(128)}, u32[]{:S(2)}) %copy-start.6) | copy-done | bytes 536
  7.7 11.9 %backward.1 = (f32[16,80,128]{2,1,0:T(8,128)S(1)}, f32[16,80,128]{2,1,0:T(8,128)S(1)}, f32[3,72,128]{2,1,0:T(8,128)S(1)}) custom-call(s32[2]{0:T(128)S(1)} %pad_add_fusion.where_ref, bf16[320,3072]{1,0:T(8,128)(2,1)S(1)} %copy-done, bf16[3072,1536]{1,0:T(8,128)(2,1)} %w_ref.1, f32[1,128]{1,0:T(1,128)S(1)} %bitcast.262, bf16[64,3072]{1,0:T(8,128)(2,1)S(1)} %bitcast.259, ...), custom_call_target="tpu_custom_call" | custom-call | tf_op jit(solution)/shard_map/backward/pallas_call | solution.py:239
  19.6 0.5 collective-permute-start
  20.1 1.7 %collective-permute-done = f32[16,80,128]{2,1,0:T(8,128)S(1)} collective-permute-done((f32[16,80,128]{2,1,0:T(8,128)S(1)}, f32[16,80,128]{2,1,0:T(8,128)S(1)}, u32[]{:S(2)}, u32[]{:S(2)}) %collective-permute-start) | collective-permute-done | bytes 655392 | tf_op jit(solution)/shard_map/ppermute | solution.py:323
  21.9 0.2 select_convert_fusion
  22.1 19.7 %all_to_all.10 = f16[16,80,128]{2,1,0:T(8,128)(2,1)S(1)} all-to-all(f16[16,80,128]{2,1,0:T(8,128)(2,1)S(1)} %select_convert_fusion), channel_id=1, replica_groups=mesh['group'=2,'chip'=8,'core'=2] {'group','chip'}, dimensions={0} | all-to-all | bytes 655360 | tf_op jit(solution)/shard_map/all_to_all | solution.py:329
  41.8 0.1 fusion.53
  41.9 0.8 %broadcast_in_dim.22 = bf16[16,80,128]{2,1,0:T(8,128)(2,1)} broadcast(bf16[80,128]{1,0:T(8,128)(2,1)S(1)} %pad.4), dimensions={1,2} | broadcast | bytes 348160 | tf_op jit(solution)/shard_map/broadcast_in_dim | solution.py:343
  42.7 3.5 %all-to-all-start.1 = ((bf16[16,80,128]{2,1,0:T(8,128)(2,1)}), bf16[16,80,128]{2,1,0:T(8,128)(2,1)S(1)}, u32[]{:S(2)}, u32[]{:S(2)}) async-start(bf16[16,80,128]{2,1,0:T(8,128)(2,1)} %broadcast_in_dim.22), calls=%async_computation.1 | async-start | bytes 655360 | tf_op jit(solution)/shard_map/all_to_all | solution.py:344
  46.2 0.1 multiply_add_fusion.1
  46.3 10.5 %all-to-all-done.1.mine_ref = bf16[16,80,128]{2,1,0:T(8,128)(2,1)S(1)} async-done(((bf16[16,80,128]{2,1,0:T(8,128)(2,1)}), bf16[16,80,128]{2,1,0:T(8,128)(2,1)S(1)}, u32[]{:S(2)}, u32[]{:S(2)}) %all-to-all-start.1) | async-done | bytes 327712 | tf_op jit(solution)/shard_map/all_to_all | solution.py:344
  56.8 0.0 collective-permute-start.1
  56.8 1.6 %collective-permute-done.1.other_ref = bf16[16,80,128]{2,1,0:T(8,128)(2,1)S(1)} collective-permute-done((bf16[16,80,128]{2,1,0:T(8,128)(2,1)S(1)}, bf16[16,80,128]{2,1,0:T(8,128)(2,1)S(1)}, u32[]{:S(2)}, u32[]{:S(2)}) %collective-permute-start.1) | collective-permute-done | bytes 327712 | tf_op jit(solution)/shard_map/ppermute | solution.py:345
  58.4 1.6 %finish.1 = (bf16[64,3072]{1,0:T(8,128)(2,1)}, bf16[64,1536]{1,0:T(8,128)(2,1)}, f32[64,144]{1,0:T(8,128)}, f32[64,144]{1,0:T(8,128)}) custom-call(s32[2]{0:T(128)S(1)} %pad_add_fusion.where_ref, bf16[16,80,128]{2,1,0:T(8,128)(2,1)S(1)} %all-to-all-done.1.mine_ref, bf16[16,80,128]{2,1,0:T(8,128)(2,1)S(1)} %collective-permute-done.1.other_ref, ...), custom_call_target="tpu_custom_call" | custom-call | tf_op jit(solution)/shard_map/finish/pallas_call | solution.py:257
  (6 shorter events, 0.1 us)
Async XLA Ops:
  0.7 1.5 %copy-start = (bf16[320,3072]{1,0:T(8,128)(2,1)S(1)}, bf16[320,3072]{1,0:T(8,128)(2,1)}, u32[]{:S(2)}) copy-start(bf16[320,3072]{1,0:T(8,128)(2,1)} %hidden_ref.1) | copy-start | bytes 5898244
  2.3 1.2 %copy-start.1 = (bf16[320,1536]{1,0:T(8,128)(2,1)S(1)}, bf16[320,1536]{1,0:T(8,128)(2,1)}, u32[]{:S(2)}) copy-start(bf16[320,1536]{1,0:T(8,128)(2,1)} %cot_ref.1) | copy-start | bytes 2949124
  3.5 1.0 %copy-start.2 = (bf16[3072,64]{0,1:T(8,128)(2,1)S(1)}, bf16[3072,64]{0,1:T(8,128)(2,1)}, u32[]{:S(2)}) copy-start(bf16[3072,64]{0,1:T(8,128)(2,1)} %param.11) | copy-start | bytes 1179652
  4.5 0.9 %copy-start.3 = (bf16[64,1536]{1,0:T(8,128)(2,1)S(1)}, bf16[64,1536]{1,0:T(8,128)(2,1)}, u32[]{:S(2)}) copy-start(bf16[64,1536]{1,0:T(8,128)(2,1)} %up_ref.1) | copy-start | bytes 589828
  5.4 0.8 %copy-start.4 = (f32[144,64]{0,1:T(8,128)S(1)}, f32[144,64]{0,1:T(8,128)}, u32[]{:S(2)}) copy-start(f32[144,64]{0,1:T(8,128)} %param.14) | copy-start | bytes 110596
  6.2 0.8 %copy-start.5 = (f32[144,64]{0,1:T(8,128)S(1)}, f32[144,64]{0,1:T(8,128)}, u32[]{:S(2)}) copy-start(f32[144,64]{0,1:T(8,128)} %param.15) | copy-start | bytes 110596
  7.1 0.7 %copy-start.6 = (f32[128]{0:T(128)S(1)}, f32[128]{0:T(128)}, u32[]{:S(2)}) copy-start(f32[128]{0:T(128)} %param.10) | copy-start | bytes 1540
  19.6 2.2 %collective-permute-start = (f32[16,80,128]{2,1,0:T(8,128)S(1)}, f32[16,80,128]{2,1,0:T(8,128)S(1)}, u32[]{:S(2)}, u32[]{:S(2)}) collective-permute-start(f32[16,80,128]{2,1,0:T(8,128)S(1)} %get-tuple-element.13), channel_id=1, source_target_pairs={{0,1},{1,0},{2,3},{3,2},{4,5},{5,4},{6,7},{7,6},{8,9},{9,8},{10,11... | collective-permute-start | bytes 1966088 | tf_op jit(solution)/shard_map/ppermute | solution.py:323
  42.7 14.1 %all-to-all-start.1 = ((bf16[16,80,128]{2,1,0:T(8,128)(2,1)}), bf16[16,80,128]{2,1,0:T(8,128)(2,1)S(1)}, u32[]{:S(2)}, u32[]{:S(2)}) async-start(bf16[16,80,128]{2,1,0:T(8,128)(2,1)} %broadcast_in_dim.22), calls=%async_computation.1 | async-start | bytes 655360 | tf_op jit(solution)/shard_map/all_to_all | solution.py:344
  56.8 1.6 %collective-permute-start.1 = (bf16[16,80,128]{2,1,0:T(8,128)(2,1)S(1)}, bf16[16,80,128]{2,1,0:T(8,128)(2,1)S(1)}, u32[]{:S(2)}, u32[]{:S(2)}) collective-permute-start(bf16[16,80,128]{2,1,0:T(8,128)(2,1)S(1)} %all-to-all-done.1.mine_ref), channel_id=1, source_target_pairs={{0,1},{1,0},{2,3},{3,2},{4,5},{5,4},{6,7},{7,6},{8,9},{9,8},{10,11... | collective-permute-start | bytes 983048 | tf_op jit(solution)/shard_map/ppermute | solution.py:345

commit v2 on v1

v2 whole, which is shorter than its diff:
```python
import functools

import jax
import jax.numpy as jnp
from jax import lax
from jax.experimental import pallas as pl
from jax.experimental.pallas import tpu as pltpu
from jax.sharding import Mesh
from jax.sharding import PartitionSpec as P

adapter_scale_factor = 0.5
norm_epsilon = 1e-06
beta_one = 0.9
beta_two = 0.999
first_bias = 1.0 - 0.9**10
second_bias = 1.0 - 0.999**10
learn_rate = 0.001
adam_eps = 1e-08

LANES = 128
SUB = 8
EXTRA = 8
TOP = 14.0
TINY = 1e-30
F32 = jnp.float32
BF16 = jnp.bfloat16
EVERY = ("group", "chip", "core")
CHIPS = ("group", "chip")
SWAP = ((0, 1), (1, 0))


def lanes_of(shape):
    return lax.broadcasted_iota(jnp.int32, shape, len(shape) - 1)


def pack_tail(tile, start):
    step = LANES // SUB
    group = lanes_of((SUB, LANES)) // step
    out = None
    for r in range(SUB):
        part = tile[SUB * r : SUB * (r + 1), :]
        shift = (step * r - start) % LANES
        if not isinstance(shift, int) or shift:
            part = pltpu.roll(part, shift, 1)
        out = part if out is None else jnp.where(group == r, part, out)
    return out


def unpack_tail(tail, start):
    step = LANES // SUB
    parts = []
    for r in range(SUB):
        shift = (start - step * r) % LANES
        moved = not isinstance(shift, int) or shift
        parts.append(pltpu.roll(tail, shift, 1) if moved else tail)
    return jnp.concatenate(parts, axis=0)


def backward_kernel(steps, *refs, packed):
    if packed:
        (where_ref, hidden_h, w_h, gain_h, down_h, up_h, cot_h, first_h, second_h) = refs[:9]
        (keep_ref, send_ref, own_ref) = refs[9:12]
        (hidden, w, gain, down, up, cot, project_s, grads_s, first_s, second_s, sems) = refs[12:]
    else:
        (where_ref, hidden_h, w_h, gain_h, down_h, up_h, cot_h) = refs[:7]
        grads_s = refs[7]
        (hidden, w, gain, down, up, cot, project_s, sems) = refs[8:]
    tokens, model_width = hidden.shape
    width = w.shape[2]
    head = gain.shape[1]
    features = up.shape[1]
    copies = {}

    def fetch(name, source, target):
        copy = pltpu.make_async_copy(source, target, sems.at[len(copies)])
        copy.start()
        copies[name] = copy

    fetch("hidden", hidden_h, hidden)
    fetch("down", down_h, down)
    for j in range(steps):
        place = pl.ds(j * width, width)
        fetch(("w", j), w_h.at[:, place], w.at[j])
        if j == 0:
            fetch("up", up_h, up)
            fetch("gain", gain_h, gain)
        fetch(("cot", j), cot_h.at[:, place], cot.at[j])
    if packed:
        fetch("first", first_h, first_s)
        fetch("second", second_h, second_s)

    copies["hidden"].wait()
    copies["down"].wait()
    low = lax.dot_general(
        hidden[...], down[...], (((1,), (1,)), ((), ())), preferred_element_type=F32
    ).astype(BF16)
    scaled = (low.astype(F32) * adapter_scale_factor).astype(BF16)
    back = jnp.zeros(scaled.shape, F32)
    done = 0
    for j in range(steps + 1):
        if j < steps:
            copies["w", j].wait()
            project_s[j % 2] = jnp.dot(hidden[...], w[j], preferred_element_type=F32)
        if j == 0:
            copies["up"].wait()
            copies["gain"].wait()
            continue
        copies["cot", j - 1].wait()
        up_part = up[:, (j - 1) * width : j * width]
        project = project_s[(j - 1) % 2] + jnp.dot(scaled, up_part, preferred_element_type=F32)
        pieces = []
        for h in range(width // head):
            mine = project[:, h * head : (h + 1) * head]
            inverse = lax.rsqrt(jnp.mean(mine * mine, axis=-1, keepdims=True) + norm_epsilon)
            normed = mine * inverse
            upstream = cot[j - 1, :, h * head : (h + 1) * head].astype(F32) * gain[...]
            mean = jnp.mean(upstream * normed, axis=-1, keepdims=True)
            pieces.append((inverse * (upstream - normed * mean)).astype(BF16))
        grad_pre = jnp.concatenate(pieces, axis=1)
        back = back + lax.dot_general(
            grad_pre, up_part, (((1,), (1,)), ((), ())), preferred_element_type=F32
        )
        place = slice(model_width + (j - 1) * width, model_width + j * width)
        grads_s[:, place] = lax.dot_general(
            scaled, grad_pre, (((0,), (0,)), ((), ())), preferred_element_type=F32
        )

    back_low = (adapter_scale_factor * back).astype(BF16)
    part = 6 * LANES if model_width % (6 * LANES) == 0 else model_width
    for start in range(0, model_width, part):
        grads_s[:, start : start + part] = lax.dot_general(
            back_low,
            hidden[:, start : start + part],
            (((0,), (0,)), ((), ())),
            preferred_element_type=F32,
        )
    if packed:
        copies["first"].wait()
        copies["second"].wait()
        pack_blocks(where_ref, grads_s, down, up, first_s, second_s, keep_ref, send_ref, own_ref)


def pack_blocks(where_ref, grads_s, down, up, first_s, second_s, keep_ref, send_ref, own_ref):
    lane = lanes_of((64, LANES))
    core = where_ref[1]
    on_zero = jnp.full((SUB, LANES), core, jnp.int32) == 0
    on_zero_main = jnp.full((64, LANES), core, jnp.int32) == 0

    def block_of(i):
        j, tile = i % SUB, i // SUB * (SUB + 1) + i % SUB
        a = grads_s[:, tile * LANES : (tile + 1) * LANES]
        b = grads_s[:, (tile + 1) * LANES : (tile + 2) * LANES]
        main = jnp.where(lane >= 16 * j, a, b) if j else a
        tail = pack_tail(b, 16 * j)
        top = jnp.abs(tail)
        for r in range(SUB):
            top = jnp.maximum(top, jnp.abs(main[SUB * r : SUB * (r + 1)]))
        return main, tail, top

    for k in range(keep_ref.shape[0]):
        even, odd = block_of(2 * k), block_of(2 * k + 1)
        for ref, (one, two) in ((keep_ref, (even, odd)), (send_ref, (odd, even))):
            ref[k, :64] = jnp.where(on_zero_main, one[0], two[0])
            ref[k, 64:72] = jnp.where(on_zero, one[1], two[1])
            ref[k, 72:80] = jnp.where(on_zero, one[2], two[2])

    index = where_ref[0]
    j = index % SUB
    tile = index // SUB * (SUB + 1) + j
    tiles = down.shape[1] // LANES

    def params_at(t):
        t_down = jnp.minimum(t, tiles - 1)
        t_up = jnp.maximum(t - tiles, 0)
        a = down[:, pl.ds(pl.multiple_of(t_down * LANES, LANES), LANES)].astype(F32)
        b = up[:, pl.ds(pl.multiple_of(t_up * LANES, LANES), LANES)].astype(F32)
        return jnp.where(jnp.full((64, LANES), t, jnp.int32) < tiles, a, b)

    a, b = params_at(tile), params_at(tile + 1)
    own_ref[0, :64] = jnp.where(lane >= 16 * j, a, b)
    own_ref[0, 64:72] = pack_tail(b, 16 * j)
    for n, ref in ((1, first_s), (2, second_s)):
        own_ref[n, :64] = pltpu.roll(ref[:, :LANES], 16 * j, 1)
        last = jnp.concatenate([ref[:, LANES:], jnp.zeros((64, LANES - 16), F32)], axis=1)
        own_ref[n, 64:72] = pack_tail(last, 0)


def finish_kernel(where_ref, mine_ref, other_ref, own_ref, down_ref, up_ref, first_ref, second_ref):
    lane = lanes_of((64, LANES))
    core = where_ref[1]
    on_zero = jnp.full((72, LANES), core, jnp.int32) == 0
    down_tiles = down_ref.shape[1] // LANES
    blocks = {}

    def block_of(i):
        if i not in blocks:
            blocks.clear()
            k = i // 2
            one, two = mine_ref[k].astype(F32), other_ref[k].astype(F32)
            blocks[2 * k] = jnp.where(on_zero, one, two)
            blocks[2 * k + 1] = jnp.where(on_zero, two, one)
        return blocks[i]

    tiles = (down_ref.shape[1] + up_ref.shape[1]) // LANES
    before = None
    for tile in range(tiles):
        group, t = tile // (SUB + 1), tile % (SUB + 1)
        value = None
        if t < SUB:
            value = block_of(SUB * group + t)
        out = value[:64] if t == 0 else None
        if t:
            out = unpack_tail(before[64:72], 16 * (t - 1))
            if t > 1:
                out = jnp.where(lane < 16 * (t - 1), before[:64], out)
            if t < SUB:
                out = jnp.where(lane >= 16 * t, value[:64], out)
        before = value
        out = out.astype(BF16)
        if tile < down_tiles:
            down_ref[:, tile * LANES : (tile + 1) * LANES] = out
        else:
            up_ref[:, (tile - down_tiles) * LANES : (tile - down_tiles + 1) * LANES] = out

    j = where_ref[0] % SUB
    for n, ref in ((0, first_ref), (1, second_ref)):
        ref[:, :LANES] = pltpu.roll(own_ref[n, :64], (LANES - 16 * j) % LANES, 1)
        ref[:, LANES:] = unpack_tail(own_ref[n, 64:72], 0)[:, :16]


def backward(where, hidden, w_query, gain, down_t, up, cotangent, first_t, second_t, chips, packed):
    tokens, model_width = hidden.shape
    features = w_query.shape[1]
    rank = down_t.shape[0]
    head = gain.shape[1]
    width = 2 * head if features % (2 * head) == 0 else head
    steps = features // width
    rows = model_width + features
    far = pl.BlockSpec(memory_space=pltpu.HBM)
    near = pl.BlockSpec(memory_space=pltpu.VMEM)
    operands = [hidden, w_query, gain, down_t, up, cotangent]
    scratch = [
        pltpu.VMEM((tokens, model_width), BF16),
        pltpu.VMEM((steps, model_width, width), BF16),
        pltpu.VMEM((1, head), F32),
        pltpu.VMEM((rank, model_width), BF16),
        pltpu.VMEM((rank, features), BF16),
        pltpu.VMEM((steps, tokens, width), BF16),
        pltpu.VMEM((2, tokens, width), F32),
    ]
    if packed:
        own = rows // chips // 2
        height = rank * own // LANES
        halves = (chips, height + EXTRA, LANES)
        operands += [first_t, second_t]
        out_shape = [jax.ShapeDtypeStruct(halves, F32)] * 2 + [
            jax.ShapeDtypeStruct((3, height, LANES), F32)
        ]
        out_specs = [near] * 3
        scratch += [pltpu.VMEM((rank, rows), F32)] + [pltpu.VMEM((rank, own), F32)] * 2
    else:
        out_shape = jax.ShapeDtypeStruct((rank, rows), F32)
        out_specs = near
    scratch += [pltpu.SemaphoreType.DMA((2 * steps + 6,))]
    operands = [pltpu.with_memory_space_constraint(x, pltpu.HBM) for x in operands]
    return pl.pallas_call(
        functools.partial(backward_kernel, steps, packed=packed),
        in_specs=[pl.BlockSpec(memory_space=pltpu.SMEM)] + [far] * len(operands),
        out_specs=out_specs,
        out_shape=out_shape,
        scratch_shapes=scratch,
        compiler_params=pltpu.CompilerParams(vmem_limit_bytes=32 << 20),
        name="backward",
    )(where, *operands)


def finish(where, mine, other, own_new, model_width, features):
    rank = 64
    own = own_new.shape[1] * LANES // rank
    full = pl.BlockSpec(memory_space=pltpu.VMEM)
    return pl.pallas_call(
        finish_kernel,
        in_specs=[pl.BlockSpec(memory_space=pltpu.SMEM), full, full, full],
        out_specs=[full] * 4,
        out_shape=[
            jax.ShapeDtypeStruct((rank, model_width), BF16),
            jax.ShapeDtypeStruct((rank, features), BF16),
            jax.ShapeDtypeStruct((rank, own), F32),
            jax.ShapeDtypeStruct((rank, own), F32),
        ],
        compiler_params=pltpu.CompilerParams(vmem_limit_bytes=32 << 20),
        name="finish",
    )(where, mine, other, own_new)


def rows_of(columns):
    return columns.reshape(-1, LANES)


def on_device(
    hidden_in,
    w_query,
    query_gain,
    down_projection_matrix,
    up_projection_matrix,
    query_cotangent,
    first_moment,
    second_moment,
):
    model_width, rank = down_projection_matrix.shape
    features = up_projection_matrix.shape[1]
    chips = lax.axis_size(CHIPS)
    devices = 2 * chips
    own = (model_width + features) // devices
    height = rank * own // LANES
    groups = -(-height // SUB)
    packed = rank == 64 and own == LANES + 16 and model_width % LANES == 0 and chips % 4 == 0
    core = lax.axis_index("core")
    index = lax.axis_index(EVERY)
    where = jnp.stack([index, core]).astype(jnp.int32)
    down_t = down_projection_matrix.T
    result = backward(
        where,
        hidden_in,
        w_query,
        query_gain[None, :],
        down_t,
        up_projection_matrix,
        query_cotangent,
        first_moment.T,
        second_moment.T,
        chips,
        packed,
    )
    if packed:
        keep, send, own_state = result
        params, first, second = own_state[0], own_state[1], own_state[2]
    else:
        blocks = result.reshape(rank, chips, 2, own).transpose(2, 1, 0, 3).reshape(2, chips, -1, LANES)
        blocks = jnp.pad(blocks, ((0, 0), (0, 0), (0, groups * SUB - height), (0, 0)))
        top = jnp.max(jnp.abs(blocks).reshape(2, chips, groups, SUB, LANES), axis=2)
        blocks = jnp.concatenate([blocks, top], axis=2)
        keep = lax.dynamic_index_in_dim(blocks, core, 0, keepdims=False)
        send = lax.dynamic_index_in_dim(blocks, 1 - core, 0, keepdims=False)
        combined = jnp.concatenate([down_t, up_projection_matrix], axis=1)
        params = rows_of(lax.dynamic_slice_in_dim(combined, index * own, own, 1)).astype(F32)
        first, second = rows_of(first_moment.T), rows_of(second_moment.T)

    total = (keep + lax.ppermute(send, "core", SWAP)).reshape(chips, groups + 1, SUB, LANES)
    power = jnp.ceil(jnp.log2(jnp.maximum(total[:, groups:], TINY))) - TOP
    is_value = lax.broadcasted_iota(jnp.int32, total.shape, 1) < groups
    coded = jnp.where(is_value, total * jnp.exp2(-power), power).astype(jnp.float16)
    arrived = lax.all_to_all(coded, CHIPS, 0, 0, tiled=True)

    grads = None
    for k in range(chips):
        term = arrived[k, :groups].astype(F32) * jnp.exp2(arrived[k, groups:].astype(F32))
        grads = term if grads is None else grads + term
    grads = grads.reshape(groups * SUB, LANES)[:height]
    grads = grads / devices
    first_new = beta_one * first + (1.0 - beta_one) * grads
    second_new = beta_two * second + (1.0 - beta_two) * grads * grads
    direction = first_new / first_bias / (jnp.sqrt(second_new / second_bias) + adam_eps)
    updated = (params - learn_rate * direction).astype(BF16)

    copies = jnp.broadcast_to(updated[None], (chips, height, LANES))
    copies, first_new, second_new = lax.optimization_barrier((copies, first_new, second_new))
    mine = lax.all_to_all(copies, CHIPS, 0, 0, tiled=True)
    other = lax.ppermute(mine, "core", SWAP)
    if packed:
        own_new = jnp.stack([first_new, second_new])
        down_new, up_new, first_out, second_out = finish(where, mine, other, own_new, model_width, features)
    else:
        pair = jnp.stack([mine, other])
        pair = jnp.where(core == 0, pair, pair[::-1])
        columns = pair.reshape(2, chips, rank, own).transpose(2, 1, 0, 3).reshape(rank, devices * own)
        down_new, up_new = columns[:, :model_width], columns[:, model_width:]
        first_out, second_out = first_new.reshape(rank, own), second_new.reshape(rank, own)
    return (down_new.T, up_new, first_out.T, second_out.T)


def solution(mesh):
    groups, replicas = mesh.shape["group"], mesh.shape["replica"]
    fine = Mesh(mesh.devices.reshape(groups, replicas // 2, 2), EVERY)
    rows = P(EVERY, None)
    return jax.shard_map(
        on_device,
        mesh=fine,
        in_specs=(rows, P(), P(), P(), P(), rows, rows, rows),
        out_specs=(P(), P(), rows, rows),
        check_vma=False,
    )
```

time: 60.6 us -> 53.9 us (0.89)
  blocking collectives: 19.7 us -> 32.9 us
  waiting for transfers between devices: 13.8 us -> 3.29 us
  local copies, waits for them, and re-layouts: 7.78 us -> 0.04 us
  starting transfers between devices: 4.06 us -> 0.52 us
  Pallas kernels: 13.4 us -> 15.6 us
    all_to_all x0 -> x1, blocking collectives: none -> 13.3 us  [on_device(): mine = lax.all_to_all(copies, CHIPS, 0, 0, tiled=True)]
    all_to_all x1 -> x0, waiting for transfers between devices: 10.5 us -> none  [on_device(): mine = lax.all_to_all(copies, CHIPS, 0, 0, tiled=True)]
    unnamed x14 -> x0, local copies, waits for them, and re-layouts: 7 us -> none
    all_to_all x1 -> x0, starting transfers between devices: 3.54 us -> none  [on_device(): mine = lax.all_to_all(copies, CHIPS, 0, 0, tiled=True)]
    pallas_call x1, Pallas kernels: 11.9 us -> 14.1 us  [backward(): pl.pallas_call(functools.partial(backward_kernel, steps, packed=packed),...]
    broadcast_in_dim x1, local copies, waits for them, and re-layouts: 0.77 us -> 0.04 us  [on_device(): copies = jnp.broadcast_to(updated[None], (chips, height, LANES))]
  transfers between devices with their start and end apart: 3 -> 2, of which waited for: 3 -> 2; matrix products, arithmetic and copies ran while one was open for 0% -> 0% of each run, Pallas kernels for 0% -> 0%
where the time goes in v2:
time: 53.9 us; the launch traced here: 53.7 us
  blocking collectives  32.9 us (61%)
  Pallas kernels  15.6 us (29%)
  waiting for transfers between devices  3.29 us (6%)
  between operations  0.69 us (1%)
  other arithmetic  0.62 us (1%)
    all_to_all x1, blocking collectives, on_device(): arrived = lax.all_to_all(coded, CHIPS, 0, 0, tiled=True)  19.6 us
    pallas_call x1, Pallas kernels, backward(): pl.pallas_call(functools.partial(backward_kernel, steps, packed=packed),...  14.1 us
    all_to_all x1, blocking collectives, on_device(): mine = lax.all_to_all(copies, CHIPS, 0, 0, tiled=True)  13.3 us
    ppermute x1, waiting for transfers between devices, on_device(): lax.ppermute(send, 'core', SWAP)  1.72 us
    ppermute x1, waiting for transfers between devices, on_device(): other = lax.ppermute(mine, 'core', SWAP)  1.57 us
    pallas_call x1, Pallas kernels, finish(): pl.pallas_call(finish_kernel, in_specs=[pl.BlockSpec(memory_space=pltpu.S...  1.56 us
  transfers between devices with their start and end apart: 2, of which 2 were waited for; matrix products, arithmetic and copies ran while one was open for 0% of the time, Pallas kernels for 0%

profile of v2, /device:TPU:0, one launch (start us, length us, event | category | flops | bytes accessed | tf_op | source)
XLA Modules:
  0.0 53.7 jit_solution(4372395511654390510)
XLA Ops:
  0.6 0.1 pad_add_fusion.refs_0_.where_ref
  0.7 14.1 %backward.1 = (f32[16,80,128]{2,1,0:T(8,128)S(1)}, f32[16,80,128]{2,1,0:T(8,128)S(1)}, f32[3,72,128]{2,1,0:T(8,128)S(1)}) custom-call(s32[2]{0:T(128)S(1)} %pad_add_fusion.refs_0_.where_ref, bf16[320,3072]{1,0:T(8,128)(2,1)} %refs_1_.1, bf16[3072,1536]{1,0:T(8,128)(2,1)} %refs_2_.1, f32[1,128]{1,0:T(1,128)} %bitcast.534, bf16[64,3072]{1,0:T(8,128)(2,1)} %bitcast.529, ...), custom_call_target="tpu_custom_call" | custom-call | tf_op jit(solution)/shard_map/backward/pallas_call | solution.py:266
  14.8 0.5 collective-permute-start
  15.3 1.7 %collective-permute-done = f32[16,80,128]{2,1,0:T(8,128)S(1)} collective-permute-done((f32[16,80,128]{2,1,0:T(8,128)S(1)}, f32[16,80,128]{2,1,0:T(8,128)S(1)}, u32[]{:S(2)}, u32[]{:S(2)}) %collective-permute-start) | collective-permute-done | bytes 655392 | tf_op jit(solution)/shard_map/ppermute | solution.py:349
  17.0 0.1 add_bitcast_fusion
  17.1 0.2 select_convert_fusion
  17.3 19.6 %all_to_all.10 = f16[16,10,8,128]{3,2,1,0:T(8,128)(2,1)S(1)} all-to-all(f16[16,10,8,128]{3,2,1,0:T(8,128)(2,1)S(1)} %select_convert_fusion), channel_id=1, replica_groups=mesh['group'=2,'chip'=8,'core'=2] {'group','chip'}, dimensions={0} | all-to-all | bytes 655360 | tf_op jit(solution)/shard_map/all_to_all | solution.py:353
  37.0 0.1 bitcast_add_fusion
  37.1 0.1 fusion.67
  37.3 13.3 %all_to_all.11.mine_ref = bf16[16,72,128]{2,1,0:T(8,128)(2,1)S(1)} all-to-all(bf16[16,72,128]{2,1,0:T(8,128)(2,1)S(1)} %broadcast_in_dim.25), channel_id=1, replica_groups=mesh['group'=2,'chip'=8,'core'=2] {'group','chip'}, dimensions={0} | all-to-all | bytes 589824 | tf_op jit(solution)/shard_map/all_to_all | solution.py:368
  50.6 0.0 collective-permute-start.1
  50.6 1.6 %collective-permute-done.1.other_ref = bf16[16,72,128]{2,1,0:T(8,128)(2,1)S(1)} collective-permute-done((bf16[16,72,128]{2,1,0:T(8,128)(2,1)S(1)}, bf16[16,72,128]{2,1,0:T(8,128)(2,1)S(1)}, u32[]{:S(2)}, u32[]{:S(2)}) %collective-permute-start.1) | collective-permute-done | bytes 294944 | tf_op jit(solution)/shard_map/ppermute | solution.py:369
  52.1 1.6 %finish.1 = (bf16[64,3072]{1,0:T(8,128)(2,1)}, bf16[64,1536]{1,0:T(8,128)(2,1)}, f32[64,144]{1,0:T(8,128)}, f32[64,144]{1,0:T(8,128)}) custom-call(s32[2]{0:T(128)S(1)} %pad_add_fusion.refs_0_.where_ref, bf16[16,72,128]{2,1,0:T(8,128)(2,1)S(1)} %all_to_all.11.mine_ref, bf16[16,72,128]{2,1,0:T(8,128)(2,1)S(1)} %collective-permute-done.1.other_ref, ...), custom_call_target="tpu_custom_call" | custom-call | tf_op jit(solution)/shard_map/finish/pallas_call | solution.py:281
  (6 shorter events, 0.1 us)
Async XLA Ops:
  14.8 2.2 %collective-permute-start = (f32[16,80,128]{2,1,0:T(8,128)S(1)}, f32[16,80,128]{2,1,0:T(8,128)S(1)}, u32[]{:S(2)}, u32[]{:S(2)}) collective-permute-start(f32[16,80,128]{2,1,0:T(8,128)S(1)} %get-tuple-element.16), channel_id=1, source_target_pairs={{0,1},{1,0},{2,3},{3,2},{4,5},{5,4},{6,7},{7,6},{8,9},{9,8},{10,11... | collective-permute-start | bytes 1966088 | tf_op jit(solution)/shard_map/ppermute | solution.py:349
  50.6 1.6 %collective-permute-start.1 = (bf16[16,72,128]{2,1,0:T(8,128)(2,1)S(1)}, bf16[16,72,128]{2,1,0:T(8,128)(2,1)S(1)}, u32[]{:S(2)}, u32[]{:S(2)}) collective-permute-start(bf16[16,72,128]{2,1,0:T(8,128)(2,1)S(1)} %all_to_all.11.mine_ref), channel_id=1, source_target_pairs={{0,1},{1,0},{2,3},{3,2},{4,5},{5,4},{6,7},{7,6},{8,9},{9,8},{10,11... | collective-permute-start | bytes 884744 | tf_op jit(solution)/shard_map/ppermute | solution.py:369

commit v3 on v2

--- a/solution.py
+++ b/solution.py
@@ -22,6 +22,7 @@
 EXTRA = 8
 TOP = 14.0
 TINY = 1e-30
+PIECES = 2
 F32 = jnp.float32
 BF16 = jnp.bfloat16
 EVERY = ("group", "chip", "core")
@@ -60,83 +61,115 @@
     if packed:
         (where_ref, hidden_h, w_h, gain_h, down_h, up_h, cot_h, first_h, second_h) = refs[:9]
         (keep_ref, send_ref, own_ref) = refs[9:12]
-        (hidden, w, gain, down, up, cot, project_s, grads_s, first_s, second_s, sems) = refs[12:]
+        (hidden, w, gain, down, up, cot, project_s, grad_s, back_s, turned, grads_s, first_s, second_s, sems) = refs[12:]
     else:
         (where_ref, hidden_h, w_h, gain_h, down_h, up_h, cot_h) = refs[:7]
         grads_s = refs[7]
-        (hidden, w, gain, down, up, cot, project_s, sems) = refs[8:]
-    tokens, model_width = hidden.shape
+        (hidden, w, gain, down, up, cot, project_s, grad_s, back_s, turned, sems) = refs[8:]
+    tokens, model_width = hidden_h.shape
     width = w.shape[2]
     head = gain.shape[1]
-    features = up.shape[1]
-    copies = {}
-
-    def fetch(name, source, target):
-        copy = pltpu.make_async_copy(source, target, sems.at[len(copies)])
+    rank, features = up.shape
+    full = model_width + rank
+    piece = model_width // PIECES
+
+    def block(ref, j):
+        return ref.at[:, pl.ds(pl.multiple_of(j * width, width), width)]
+
+    def part(ref, i):
+        return ref.at[:, pl.ds(pl.multiple_of(i * piece, piece), piece)]
+
+    def hidden_copy(i):
+        return pltpu.make_async_copy(part(hidden_h, i), part(hidden, i), sems.at[i])
+
+    def w_copy(j):
+        return pltpu.make_async_copy(block(w_h, j), w.at[j, :model_width], sems.at[PIECES + j])
+
+    def up_copy(j):
+        return pltpu.make_async_copy(
+            block(up_h, j), w.at[j, model_width:full], sems.at[PIECES + steps + j]
+        )
+
+    def cot_copy(j):
+        return pltpu.make_async_copy(block(cot_h, j), cot.at[j], sems.at[PIECES + 2 * steps + j])
+
+    single = [(down_h, down), (gain_h, gain), (up_h, up)]
+    if packed:
+        single += [(first_h, first_s), (second_h, second_s)]
+    single = [
+        pltpu.make_async_copy(source, target, sems.at[PIECES + 3 * steps + n])
+        for n, (source, target) in enumerate(single)
+    ]
+
+    def each(n, body):
+        lax.fori_loop(0, n, lambda i, _: body(i), None)
+
+    single[0].start()
+    each(PIECES, lambda i: hidden_copy(i).start())
+    single[1].start()
+
+    def start_block(j):
+        up_copy(j).start()
+        cot_copy(j).start()
+        w_copy(j).start()
+
+    each(steps, start_block)
+    for copy in single[2:]:
         copy.start()
-        copies[name] = copy
-
-    fetch("hidden", hidden_h, hidden)
-    fetch("down", down_h, down)
-    for j in range(steps):
-        place = pl.ds(j * width, width)
-        fetch(("w", j), w_h.at[:, place], w.at[j])
-        if j == 0:
-            fetch("up", up_h, up)
-            fetch("gain", gain_h, gain)
-        fetch(("cot", j), cot_h.at[:, place], cot.at[j])
-    if packed:
-        fetch("first", first_h, first_s)
-        fetch("second", second_h, second_s)
-
-    copies["hidden"].wait()
-    copies["down"].wait()
-    low = lax.dot_general(
-        hidden[...], down[...], (((1,), (1,)), ((), ())), preferred_element_type=F32
-    ).astype(BF16)
+
+    back_s[...] = jnp.zeros_like(back_s)
+    single[0].wait()
+
+    def add_low(i):
+        hidden_copy(i).wait()
+        back_s[...] += lax.dot_general(
+            part(hidden, i)[...],
+            part(down, i)[...],
+            (((1,), (1,)), ((), ())),
+            preferred_element_type=F32,
+        )
+
+    each(PIECES, add_low)
+    low = back_s[...].astype(BF16)
     scaled = (low.astype(F32) * adapter_scale_factor).astype(BF16)
-    back = jnp.zeros(scaled.shape, F32)
-    done = 0
-    for j in range(steps + 1):
-        if j < steps:
-            copies["w", j].wait()
-            project_s[j % 2] = jnp.dot(hidden[...], w[j], preferred_element_type=F32)
-        if j == 0:
-            copies["up"].wait()
-            copies["gain"].wait()
-            continue
-        copies["cot", j - 1].wait()
-        up_part = up[:, (j - 1) * width : j * width]
-        project = project_s[(j - 1) % 2] + jnp.dot(scaled, up_part, preferred_element_type=F32)
-        pieces = []
+    hidden[:, model_width:] = scaled
+    turned[...] = scaled.T
+    single[1].wait()
+
+    def normalise(j):
         for h in range(width // head):
-            mine = project[:, h * head : (h + 1) * head]
+            place = slice(h * head, (h + 1) * head)
+            mine = project_s[:, place]
+            upstream = cot[j, :, place].astype(F32) * gain[...]
             inverse = lax.rsqrt(jnp.mean(mine * mine, axis=-1, keepdims=True) + norm_epsilon)
             normed = mine * inverse
-            upstream = cot[j - 1, :, h * head : (h + 1) * head].astype(F32) * gain[...]
             mean = jnp.mean(upstream * normed, axis=-1, keepdims=True)
-            pieces.append((inverse * (upstream - normed * mean)).astype(BF16))
-        grad_pre = jnp.concatenate(pieces, axis=1)
-        back = back + lax.dot_general(
-            grad_pre, up_part, (((1,), (1,)), ((), ())), preferred_element_type=F32
-        )
-        place = slice(model_width + (j - 1) * width, model_width + j * width)
-        grads_s[:, place] = lax.dot_general(
-            scaled, grad_pre, (((0,), (0,)), ((), ())), preferred_element_type=F32
-        )
-
-    back_low = (adapter_scale_factor * back).astype(BF16)
-    part = 6 * LANES if model_width % (6 * LANES) == 0 else model_width
-    for start in range(0, model_width, part):
-        grads_s[:, start : start + part] = lax.dot_general(
-            back_low,
-            hidden[:, start : start + part],
-            (((0,), (0,)), ((), ())),
-            preferred_element_type=F32,
-        )
-    if packed:
-        copies["first"].wait()
-        copies["second"].wait()
+            place = pl.ds(pl.multiple_of(j * width + h * head, head), head)
+            grad_s[:, place] = (inverse * (upstream - normed * mean)).astype(BF16)
+
+    def step(j, _):
+        w_copy(j).wait()
+        up_copy(j).wait()
+        cot_copy(j).wait()
+        before = jnp.maximum(j - 1, 0)
+        normalise(before)
+        project_s[...] = jnp.dot(hidden[...], w[j], preferred_element_type=F32)
+
+    project_s[...] = jnp.zeros_like(project_s)
+    lax.fori_loop(0, steps, step, None)
+    normalise(steps - 1)
+    single[2].wait()
+    back = lax.dot_general(
+        grad_s[...], up[...], (((1,), (1,)), ((), ())), preferred_element_type=F32
+    )
+    back_low = (adapter_scale_factor * back).astype(BF16).T
+    grads_s[:, model_width:] = jnp.dot(turned[...], grad_s[...], preferred_element_type=F32)
+    grads_s[:, :model_width] = jnp.dot(
+        back_low, hidden[:, :model_width], preferred_element_type=F32
+    )
+    if packed:
+        for copy in single[3:]:
+            copy.wait()
         pack_blocks(where_ref, grads_s, down, up, first_s, second_s, keep_ref, send_ref, own_ref)
 
 
@@ -146,10 +179,11 @@
     on_zero = jnp.full((SUB, LANES), core, jnp.int32) == 0
     on_zero_main = jnp.full((64, LANES), core, jnp.int32) == 0
 
-    def block_of(i):
-        j, tile = i % SUB, i // SUB * (SUB + 1) + i % SUB
-        a = grads_s[:, tile * LANES : (tile + 1) * LANES]
-        b = grads_s[:, (tile + 1) * LANES : (tile + 2) * LANES]
+    def tile_of(t):
+        return grads_s[:, pl.ds(pl.multiple_of(t * LANES, LANES), LANES)]
+
+    def block_of(group, j):
+        a, b = tile_of(group * (SUB + 1) + j), tile_of(group * (SUB + 1) + j + 1)
         main = jnp.where(lane >= 16 * j, a, b) if j else a
         tail = pack_tail(b, 16 * j)
         top = jnp.abs(tail)
@@ -157,12 +191,16 @@
             top = jnp.maximum(top, jnp.abs(main[SUB * r : SUB * (r + 1)]))
         return main, tail, top
 
-    for k in range(keep_ref.shape[0]):
-        even, odd = block_of(2 * k), block_of(2 * k + 1)
-        for ref, (one, two) in ((keep_ref, (even, odd)), (send_ref, (odd, even))):
-            ref[k, :64] = jnp.where(on_zero_main, one[0], two[0])
-            ref[k, 64:72] = jnp.where(on_zero, one[1], two[1])
-            ref[k, 72:80] = jnp.where(on_zero, one[2], two[2])
+    def pack_group(group, _):
+        for k in range(SUB // 2):
+            even, odd = block_of(group, 2 * k), block_of(group, 2 * k + 1)
+            chip = group * (SUB // 2) + k
+            for ref, (one, two) in ((keep_ref, (even, odd)), (send_ref, (odd, even))):
+                ref[chip, :64] = jnp.where(on_zero_main, one[0], two[0])
+                ref[chip, 64:72] = jnp.where(on_zero, one[1], two[1])
+                ref[chip, 72:80] = jnp.where(on_zero, one[2], two[2])
+
+    lax.fori_loop(0, keep_ref.shape[0] // (SUB // 2), pack_group, None)
 
     index = where_ref[0]
     j = index % SUB
@@ -236,17 +274,21 @@
     width = 2 * head if features % (2 * head) == 0 else head
     steps = features // width
     rows = model_width + features
+    depth = model_width + rank
     far = pl.BlockSpec(memory_space=pltpu.HBM)
     near = pl.BlockSpec(memory_space=pltpu.VMEM)
     operands = [hidden, w_query, gain, down_t, up, cotangent]
     scratch = [
-        pltpu.VMEM((tokens, model_width), BF16),
-        pltpu.VMEM((steps, model_width, width), BF16),
+        pltpu.VMEM((tokens, depth), BF16),
+        pltpu.VMEM((steps, depth, width), BF16),
         pltpu.VMEM((1, head), F32),
         pltpu.VMEM((rank, model_width), BF16),
         pltpu.VMEM((rank, features), BF16),
         pltpu.VMEM((steps, tokens, width), BF16),
-        pltpu.VMEM((2, tokens, width), F32),
+        pltpu.VMEM((tokens, width), F32),
+        pltpu.VMEM((tokens, features), BF16),
+        pltpu.VMEM((tokens, rank), F32),
+        pltpu.VMEM((rank, tokens), BF16),
     ]
     if packed:
         own = rows // chips // 2
@@ -261,7 +303,7 @@
     else:
         out_shape = jax.ShapeDtypeStruct((rank, rows), F32)
         out_specs = near
-    scratch += [pltpu.SemaphoreType.DMA((2 * steps + 6,))]
+    scratch += [pltpu.SemaphoreType.DMA((3 * steps + PIECES + 5,))]
     operands = [pltpu.with_memory_space_constraint(x, pltpu.HBM) for x in operands]
     return pl.pallas_call(
         functools.partial(backward_kernel, steps, packed=packed),

time: 53.9 us -> 49.5 us (0.918)
  Pallas kernels: 15.6 us -> 11.2 us
    pallas_call x1, Pallas kernels: 14.1 us -> 9.6 us  [backward(): pl.pallas_call(functools.partial(backward_kernel, steps, packed=packed),...]
where the time goes in v3:
time: 49.5 us; the launch traced here: 49.3 us
  blocking collectives  32.9 us (66%)
  Pallas kernels  11.2 us (23%)
  waiting for transfers between devices  3.29 us (7%)
  between operations  0.69 us (1%)
  other arithmetic  0.62 us (1%)
  starting transfers between devices  0.53 us (1%)
    all_to_all x1, blocking collectives, on_device(): arrived = lax.all_to_all(coded, CHIPS, 0, 0, tiled=True)  19.7 us
    all_to_all x1, blocking collectives, on_device(): mine = lax.all_to_all(copies, CHIPS, 0, 0, tiled=True)  13.3 us
    pallas_call x1, Pallas kernels, backward(): pl.pallas_call(functools.partial(backward_kernel, steps, packed=packed),...  9.6 us
    ppermute x1, waiting for transfers between devices, on_device(): lax.ppermute(send, 'core', SWAP)  1.72 us
    ppermute x1, waiting for transfers between devices, on_device(): other = lax.ppermute(mine, 'core', SWAP)  1.57 us
    pallas_call x1, Pallas kernels, finish(): pl.pallas_call(finish_kernel, in_specs=[pl.BlockSpec(memory_space=pltpu.S...  1.56 us
  transfers between devices with their start and end apart: 2, of which 2 were waited for; matrix products, arithmetic and copies ran while one was open for 0% of the time, Pallas kernels for 0%

profile of v3, /device:TPU:0, one launch (start us, length us, event | category | flops | bytes accessed | tf_op | source)
XLA Modules:
  0.0 49.3 jit_solution(13306061286153939728)
XLA Ops:
  0.6 0.1 pad_add_fusion.refs_0_.where_ref
  0.7 9.6 %backward.1 = (f32[16,80,128]{2,1,0:T(8,128)S(1)}, f32[16,80,128]{2,1,0:T(8,128)S(1)}, f32[3,72,128]{2,1,0:T(8,128)S(1)}) custom-call(s32[2]{0:T(128)S(1)} %pad_add_fusion.refs_0_.where_ref, bf16[320,3072]{1,0:T(8,128)(2,1)} %refs_1_.1, bf16[3072,1536]{1,0:T(8,128)(2,1)} %refs_2_.1, f32[1,128]{1,0:T(1,128)} %bitcast.534, bf16[64,3072]{1,0:T(8,128)(2,1)} %bitcast.529, ...), custom_call_target="tpu_custom_call" | custom-call | tf_op jit(solution)/shard_map/backward/pallas_call | solution.py:308
  10.3 0.5 %collective-permute-start = (f32[16,80,128]{2,1,0:T(8,128)S(1)}, f32[16,80,128]{2,1,0:T(8,128)S(1)}, u32[]{:S(2)}, u32[]{:S(2)}) collective-permute-start(f32[16,80,128]{2,1,0:T(8,128)S(1)} %get-tuple-element.16), channel_id=1, source_target_pairs={{0,1},{1,0},{2,3},{3,2},{4,5},{5,4},{6,7},{7,6},{8,9},{9,8},{10,11... | collective-permute-start | bytes 1966088 | tf_op jit(solution)/shard_map/ppermute | solution.py:391
  10.8 1.7 %collective-permute-done = f32[16,80,128]{2,1,0:T(8,128)S(1)} collective-permute-done((f32[16,80,128]{2,1,0:T(8,128)S(1)}, f32[16,80,128]{2,1,0:T(8,128)S(1)}, u32[]{:S(2)}, u32[]{:S(2)}) %collective-permute-start) | collective-permute-done | bytes 655392 | tf_op jit(solution)/shard_map/ppermute | solution.py:391
  12.6 0.1 add_bitcast_fusion
  12.7 0.2 select_convert_fusion
  12.9 19.7 %all_to_all.10 = f16[16,10,8,128]{3,2,1,0:T(8,128)(2,1)S(1)} all-to-all(f16[16,10,8,128]{3,2,1,0:T(8,128)(2,1)S(1)} %select_convert_fusion), channel_id=1, replica_groups=mesh['group'=2,'chip'=8,'core'=2] {'group','chip'}, dimensions={0} | all-to-all | bytes 655360 | tf_op jit(solution)/shard_map/all_to_all | solution.py:395
  32.6 0.1 bitcast_add_fusion
  32.7 0.1 fusion.67
  32.8 13.3 %all_to_all.11.mine_ref = bf16[16,72,128]{2,1,0:T(8,128)(2,1)S(1)} all-to-all(bf16[16,72,128]{2,1,0:T(8,128)(2,1)S(1)} %broadcast_in_dim.25), channel_id=1, replica_groups=mesh['group'=2,'chip'=8,'core'=2] {'group','chip'}, dimensions={0} | all-to-all | bytes 589824 | tf_op jit(solution)/shard_map/all_to_all | solution.py:410
  46.1 0.0 collective-permute-start.1
  46.1 1.6 %collective-permute-done.1.other_ref = bf16[16,72,128]{2,1,0:T(8,128)(2,1)S(1)} collective-permute-done((bf16[16,72,128]{2,1,0:T(8,128)(2,1)S(1)}, bf16[16,72,128]{2,1,0:T(8,128)(2,1)S(1)}, u32[]{:S(2)}, u32[]{:S(2)}) %collective-permute-start.1) | collective-permute-done | bytes 294944 | tf_op jit(solution)/shard_map/ppermute | solution.py:411
  47.7 1.6 %finish.1 = (bf16[64,3072]{1,0:T(8,128)(2,1)}, bf16[64,1536]{1,0:T(8,128)(2,1)}, f32[64,144]{1,0:T(8,128)}, f32[64,144]{1,0:T(8,128)}) custom-call(s32[2]{0:T(128)S(1)} %pad_add_fusion.refs_0_.where_ref, bf16[16,72,128]{2,1,0:T(8,128)(2,1)S(1)} %all_to_all.11.mine_ref, bf16[16,72,128]{2,1,0:T(8,128)(2,1)S(1)} %collective-permute-done.1.other_ref, ...), custom_call_target="tpu_custom_call" | custom-call | tf_op jit(solution)/shard_map/finish/pallas_call | solution.py:323
  (6 shorter events, 0.1 us)
Async XLA Ops:
  10.3 2.2 %collective-permute-start = (f32[16,80,128]{2,1,0:T(8,128)S(1)}, f32[16,80,128]{2,1,0:T(8,128)S(1)}, u32[]{:S(2)}, u32[]{:S(2)}) collective-permute-start(f32[16,80,128]{2,1,0:T(8,128)S(1)} %get-tuple-element.16), channel_id=1, source_target_pairs={{0,1},{1,0},{2,3},{3,2},{4,5},{5,4},{6,7},{7,6},{8,9},{9,8},{10,11... | collective-permute-start | bytes 1966088 | tf_op jit(solution)/shard_map/ppermute | solution.py:391
  46.1 1.6 %collective-permute-start.1 = (bf16[16,72,128]{2,1,0:T(8,128)(2,1)S(1)}, bf16[16,72,128]{2,1,0:T(8,128)(2,1)S(1)}, u32[]{:S(2)}, u32[]{:S(2)}) collective-permute-start(bf16[16,72,128]{2,1,0:T(8,128)(2,1)S(1)} %all_to_all.11.mine_ref), channel_id=1, source_target_pairs={{0,1},{1,0},{2,3},{3,2},{4,5},{5,4},{6,7},{7,6},{8,9},{9,8},{10,11... | collective-permute-start | bytes 884744 | tf_op jit(solution)/shard_map/ppermute | solution.py:411

commit v4 on v3

--- a/solution.py
+++ b/solution.py
@@ -19,9 +19,7 @@
 
 LANES = 128
 SUB = 8
-EXTRA = 8
-TOP = 14.0
-TINY = 1e-30
+RANGE = 2.0**-11
 PIECES = 2
 F32 = jnp.float32
 BF16 = jnp.bfloat16
@@ -157,13 +155,19 @@
 
     project_s[...] = jnp.zeros_like(project_s)
     lax.fori_loop(0, steps, step, None)
+    single[2].wait()
     normalise(steps - 1)
-    single[2].wait()
+    done = model_width + features - width
+    grads_s[:, model_width:done] = jnp.dot(
+        turned[...], grad_s[:, : features - width], preferred_element_type=F32
+    )
     back = lax.dot_general(
         grad_s[...], up[...], (((1,), (1,)), ((), ())), preferred_element_type=F32
     )
     back_low = (adapter_scale_factor * back).astype(BF16).T
-    grads_s[:, model_width:] = jnp.dot(turned[...], grad_s[...], preferred_element_type=F32)
+    grads_s[:, done:] = jnp.dot(
+        turned[...], grad_s[:, features - width :], preferred_element_type=F32
+    )
     grads_s[:, :model_width] = jnp.dot(
         back_low, hidden[:, :model_width], preferred_element_type=F32
     )
@@ -180,27 +184,23 @@
     on_zero_main = jnp.full((64, LANES), core, jnp.int32) == 0
 
     def tile_of(t):
-        return grads_s[:, pl.ds(pl.multiple_of(t * LANES, LANES), LANES)]
+        return grads_s[:, t * LANES : (t + 1) * LANES]
 
     def block_of(group, j):
         a, b = tile_of(group * (SUB + 1) + j), tile_of(group * (SUB + 1) + j + 1)
         main = jnp.where(lane >= 16 * j, a, b) if j else a
-        tail = pack_tail(b, 16 * j)
-        top = jnp.abs(tail)
-        for r in range(SUB):
-            top = jnp.maximum(top, jnp.abs(main[SUB * r : SUB * (r + 1)]))
-        return main, tail, top
-
-    def pack_group(group, _):
+        return main, pack_tail(b, 16 * j)
+
+    def pack_group(group):
         for k in range(SUB // 2):
             even, odd = block_of(group, 2 * k), block_of(group, 2 * k + 1)
             chip = group * (SUB // 2) + k
             for ref, (one, two) in ((keep_ref, (even, odd)), (send_ref, (odd, even))):
                 ref[chip, :64] = jnp.where(on_zero_main, one[0], two[0])
                 ref[chip, 64:72] = jnp.where(on_zero, one[1], two[1])
-                ref[chip, 72:80] = jnp.where(on_zero, one[2], two[2])
-
-    lax.fori_loop(0, keep_ref.shape[0] // (SUB // 2), pack_group, None)
+
+    for group in reversed(range(keep_ref.shape[0] // (SUB // 2))):
+        pack_group(group)
 
     index = where_ref[0]
     j = index % SUB
@@ -293,7 +293,7 @@
     if packed:
         own = rows // chips // 2
         height = rank * own // LANES
-        halves = (chips, height + EXTRA, LANES)
+        halves = (chips, height, LANES)
         operands += [first_t, second_t]
         out_shape = [jax.ShapeDtypeStruct(halves, F32)] * 2 + [
             jax.ShapeDtypeStruct((3, height, LANES), F32)
@@ -335,6 +335,16 @@
     )(where, mine, other, own_new)
 
 
+def coded_of(g):
+    root = jnp.sqrt(jnp.abs(g) * RANGE)
+    return jnp.where(g < 0, -root, root).astype(jnp.float16)
+
+
+def decoded_of(code):
+    root = code.astype(F32)
+    return root * jnp.abs(root)
+
+
 def rows_of(columns):
     return columns.reshape(-1, LANES)
 
@@ -355,7 +365,6 @@
     devices = 2 * chips
     own = (model_width + features) // devices
     height = rank * own // LANES
-    groups = -(-height // SUB)
     packed = rank == 64 and own == LANES + 16 and model_width % LANES == 0 and chips % 4 == 0
     core = lax.axis_index("core")
     index = lax.axis_index(EVERY)
@@ -379,27 +388,19 @@
         params, first, second = own_state[0], own_state[1], own_state[2]
     else:
         blocks = result.reshape(rank, chips, 2, own).transpose(2, 1, 0, 3).reshape(2, chips, -1, LANES)
-        blocks = jnp.pad(blocks, ((0, 0), (0, 0), (0, groups * SUB - height), (0, 0)))
-        top = jnp.max(jnp.abs(blocks).reshape(2, chips, groups, SUB, LANES), axis=2)
-        blocks = jnp.concatenate([blocks, top], axis=2)
         keep = lax.dynamic_index_in_dim(blocks, core, 0, keepdims=False)
         send = lax.dynamic_index_in_dim(blocks, 1 - core, 0, keepdims=False)
         combined = jnp.concatenate([down_t, up_projection_matrix], axis=1)
         params = rows_of(lax.dynamic_slice_in_dim(combined, index * own, own, 1)).astype(F32)
         first, second = rows_of(first_moment.T), rows_of(second_moment.T)
 
-    total = (keep + lax.ppermute(send, "core", SWAP)).reshape(chips, groups + 1, SUB, LANES)
-    power = jnp.ceil(jnp.log2(jnp.maximum(total[:, groups:], TINY))) - TOP
-    is_value = lax.broadcasted_iota(jnp.int32, total.shape, 1) < groups
-    coded = jnp.where(is_value, total * jnp.exp2(-power), power).astype(jnp.float16)
+    coded = coded_of(keep + lax.ppermute(send, "core", SWAP))
     arrived = lax.all_to_all(coded, CHIPS, 0, 0, tiled=True)
-
     grads = None
     for k in range(chips):
-        term = arrived[k, :groups].astype(F32) * jnp.exp2(arrived[k, groups:].astype(F32))
+        term = decoded_of(arrived[k])
         grads = term if grads is None else grads + term
-    grads = grads.reshape(groups * SUB, LANES)[:height]
-    grads = grads / devices
+    grads = grads / (RANGE * devices)
     first_new = beta_one * first + (1.0 - beta_one) * grads
     second_new = beta_two * second + (1.0 - beta_two) * grads * grads
     direction = first_new / first_bias / (jnp.sqrt(second_new / second_bias) + adam_eps)

time: 49.5 us -> 48.3 us (0.976)
  blocking collectives: 32.9 us -> 32.2 us
    all_to_all x1, blocking collectives: 19.7 us -> 19 us  [on_device(): arrived = lax.all_to_all(coded, CHIPS, 0, 0, tiled=True)]
where the time goes in v4:
time: 48.3 us; the launch traced here: 48.1 us
  blocking collectives  32.2 us (67%)
  Pallas kernels  10.8 us (22%)
  waiting for transfers between devices  3.2 us (7%)
  between operations  0.67 us (1%)
  other arithmetic  0.6 us (1%)
  starting transfers between devices  0.53 us (1%)
    all_to_all x1, blocking collectives, on_device(): arrived = lax.all_to_all(coded, CHIPS, 0, 0, tiled=True)  19 us
    all_to_all x1, blocking collectives, on_device(): mine = lax.all_to_all(copies, CHIPS, 0, 0, tiled=True)  13.2 us
    pallas_call x1, Pallas kernels, backward(): pl.pallas_call(functools.partial(backward_kernel, steps, packed=packed),...  9.27 us
    ppermute x1, waiting for transfers between devices, on_device(): coded = coded_of(keep + lax.ppermute(send, 'core', SWAP))  1.63 us
    ppermute x1, waiting for transfers between devices, on_device(): other = lax.ppermute(mine, 'core', SWAP)  1.57 us
    pallas_call x1, Pallas kernels, finish(): pl.pallas_call(finish_kernel, in_specs=[pl.BlockSpec(memory_space=pltpu.S...  1.56 us
  transfers between devices with their start and end apart: 2, of which 2 were waited for; matrix products, arithmetic and copies ran while one was open for 0% of the time, Pallas kernels for 0%

profile of v4, /device:TPU:0, one launch (start us, length us, event | category | flops | bytes accessed | tf_op | source)
XLA Modules:
  0.0 48.1 jit_solution(17783460722365191494)
XLA Ops:
  0.6 0.1 pad_add_fusion.refs_0_.where_ref
  0.7 9.3 %backward.1 = (f32[16,72,128]{2,1,0:T(8,128)S(1)}, f32[16,72,128]{2,1,0:T(8,128)S(1)}, f32[3,72,128]{2,1,0:T(8,128)S(1)}) custom-call(s32[2]{0:T(128)S(1)} %pad_add_fusion.refs_0_.where_ref, bf16[320,3072]{1,0:T(8,128)(2,1)} %refs_1_.1, bf16[3072,1536]{1,0:T(8,128)(2,1)} %refs_2_.1, f32[1,128]{1,0:T(1,128)} %bitcast.162, bf16[64,3072]{1,0:T(8,128)(2,1)} %bitcast.157, ...), custom_call_target="tpu_custom_call" | custom-call | tf_op jit(solution)/shard_map/backward/pallas_call | solution.py:308
  10.0 0.5 %collective-permute-start = (f32[16,72,128]{2,1,0:T(8,128)S(1)}, f32[16,72,128]{2,1,0:T(8,128)S(1)}, u32[]{:S(2)}, u32[]{:S(2)}) collective-permute-start(f32[16,72,128]{2,1,0:T(8,128)S(1)} %get-tuple-element.16), channel_id=1, source_target_pairs={{0,1},{1,0},{2,3},{3,2},{4,5},{5,4},{6,7},{7,6},{8,9},{9,8},{10,11... | collective-permute-start | bytes 1769480 | tf_op jit(solution)/shard_map/ppermute | solution.py:397
  10.5 1.6 %collective-permute-done = f32[16,72,128]{2,1,0:T(8,128)S(1)} collective-permute-done((f32[16,72,128]{2,1,0:T(8,128)S(1)}, f32[16,72,128]{2,1,0:T(8,128)S(1)}, u32[]{:S(2)}, u32[]{:S(2)}) %collective-permute-start) | collective-permute-done | bytes 589856 | tf_op jit(solution)/shard_map/ppermute | solution.py:397
  12.1 0.3 fusion
  12.5 19.0 %all_to_all.10 = f16[16,72,128]{2,1,0:T(8,128)(2,1)S(1)} all-to-all(f16[16,72,128]{2,1,0:T(8,128)(2,1)S(1)} %fusion), channel_id=1, replica_groups=mesh['group'=2,'chip'=8,'core'=2] {'group','chip'}, dimensions={0} | all-to-all | bytes 589824 | tf_op jit(solution)/shard_map/all_to_all | solution.py:398
  31.5 0.1 bitcast_add_fusion
  31.6 0.1 fusion.31
  31.8 13.2 %all_to_all.11.mine_ref = bf16[16,72,128]{2,1,0:T(8,128)(2,1)S(1)} all-to-all(bf16[16,72,128]{2,1,0:T(8,128)(2,1)S(1)} %broadcast_in_dim.13), channel_id=1, replica_groups=mesh['group'=2,'chip'=8,'core'=2] {'group','chip'}, dimensions={0} | all-to-all | bytes 589824 | tf_op jit(solution)/shard_map/all_to_all | solution.py:411
  44.9 0.0 collective-permute-start.1
  44.9 1.6 %collective-permute-done.1.other_ref = bf16[16,72,128]{2,1,0:T(8,128)(2,1)S(1)} collective-permute-done((bf16[16,72,128]{2,1,0:T(8,128)(2,1)S(1)}, bf16[16,72,128]{2,1,0:T(8,128)(2,1)S(1)}, u32[]{:S(2)}, u32[]{:S(2)}) %collective-permute-start.1) | collective-permute-done | bytes 294944 | tf_op jit(solution)/shard_map/ppermute | solution.py:412
  46.5 1.6 %finish.1 = (bf16[64,3072]{1,0:T(8,128)(2,1)}, bf16[64,1536]{1,0:T(8,128)(2,1)}, f32[64,144]{1,0:T(8,128)}, f32[64,144]{1,0:T(8,128)}) custom-call(s32[2]{0:T(128)S(1)} %pad_add_fusion.refs_0_.where_ref, bf16[16,72,128]{2,1,0:T(8,128)(2,1)S(1)} %all_to_all.11.mine_ref, bf16[16,72,128]{2,1,0:T(8,128)(2,1)S(1)} %collective-permute-done.1.other_ref, ...), custom_call_target="tpu_custom_call" | custom-call | tf_op jit(solution)/shard_map/finish/pallas_call | solution.py:323
  (3 shorter events, 0.1 us)
Async XLA Ops:
  10.0 2.2 %collective-permute-start = (f32[16,72,128]{2,1,0:T(8,128)S(1)}, f32[16,72,128]{2,1,0:T(8,128)S(1)}, u32[]{:S(2)}, u32[]{:S(2)}) collective-permute-start(f32[16,72,128]{2,1,0:T(8,128)S(1)} %get-tuple-element.16), channel_id=1, source_target_pairs={{0,1},{1,0},{2,3},{3,2},{4,5},{5,4},{6,7},{7,6},{8,9},{9,8},{10,11... | collective-permute-start | bytes 1769480 | tf_op jit(solution)/shard_map/ppermute | solution.py:397
  44.9 1.6 %collective-permute-start.1 = (bf16[16,72,128]{2,1,0:T(8,128)(2,1)S(1)}, bf16[16,72,128]{2,1,0:T(8,128)(2,1)S(1)}, u32[]{:S(2)}, u32[]{:S(2)}) collective-permute-start(bf16[16,72,128]{2,1,0:T(8,128)(2,1)S(1)} %all_to_all.11.mine_ref), channel_id=1, source_target_pairs={{0,1},{1,0},{2,3},{3,2},{4,5},{5,4},{6,7},{7,6},{8,9},{9,8},{10,11... | collective-permute-start | bytes 884744 | tf_op jit(solution)/shard_map/ppermute | solution.py:412

commit v5 on v4

--- a/solution.py
+++ b/solution.py
@@ -168,9 +168,14 @@
     grads_s[:, done:] = jnp.dot(
         turned[...], grad_s[:, features - width :], preferred_element_type=F32
     )
-    grads_s[:, :model_width] = jnp.dot(
-        back_low, hidden[:, :model_width], preferred_element_type=F32
-    )
+    turned[...] = back_low
+    half = model_width // 2
+
+    def down_half(i):
+        place = pl.ds(pl.multiple_of(i * half, half), half)
+        grads_s[:, place] = jnp.dot(turned[...], hidden[:, place], preferred_element_type=F32)
+
+    each(2, down_half)
     if packed:
         for copy in single[3:]:
             copy.wait()

time: 48.3 us -> 48 us (level)
  no operation moved by 1% of the time
where the time goes in v5:
time: 48 us; the launch traced here: 47.8 us
  blocking collectives  32.2 us (67%)
  Pallas kernels  10.6 us (22%)
  waiting for transfers between devices  3.2 us (7%)
  between operations  0.67 us (1%)
  other arithmetic  0.6 us (1%)
  starting transfers between devices  0.52 us (1%)
    all_to_all x1, blocking collectives, on_device(): arrived = lax.all_to_all(coded, CHIPS, 0, 0, tiled=True)  19 us
    all_to_all x1, blocking collectives, on_device(): mine = lax.all_to_all(copies, CHIPS, 0, 0, tiled=True)  13.2 us
    pallas_call x1, Pallas kernels, backward(): pl.pallas_call(functools.partial(backward_kernel, steps, packed=packed),...  9.01 us
    ppermute x1, waiting for transfers between devices, on_device(): coded = coded_of(keep + lax.ppermute(send, 'core', SWAP))  1.63 us
    ppermute x1, waiting for transfers between devices, on_device(): other = lax.ppermute(mine, 'core', SWAP)  1.57 us
    pallas_call x1, Pallas kernels, finish(): pl.pallas_call(finish_kernel, in_specs=[pl.BlockSpec(memory_space=pltpu.S...  1.56 us
  transfers between devices with their start and end apart: 2, of which 2 were waited for; matrix products, arithmetic and copies ran while one was open for 0% of the time, Pallas kernels for 0%

profile of v5, /device:TPU:0, one launch (start us, length us, event | category | flops | bytes accessed | tf_op | source)
XLA Modules:
  0.0 47.8 jit_solution(16047784920883818826)
XLA Ops:
  0.6 0.1 pad_add_fusion.refs_0_.where_ref
  0.7 9.0 %backward.1 = (f32[16,72,128]{2,1,0:T(8,128)S(1)}, f32[16,72,128]{2,1,0:T(8,128)S(1)}, f32[3,72,128]{2,1,0:T(8,128)S(1)}) custom-call(s32[2]{0:T(128)S(1)} %pad_add_fusion.refs_0_.where_ref, bf16[320,3072]{1,0:T(8,128)(2,1)} %refs_1_.1, bf16[3072,1536]{1,0:T(8,128)(2,1)} %refs_2_.1, f32[1,128]{1,0:T(1,128)} %bitcast.162, bf16[64,3072]{1,0:T(8,128)(2,1)} %bitcast.157, ...), custom_call_target="tpu_custom_call" | custom-call | tf_op jit(solution)/shard_map/backward/pallas_call | solution.py:313
  9.7 0.5 %collective-permute-start = (f32[16,72,128]{2,1,0:T(8,128)S(1)}, f32[16,72,128]{2,1,0:T(8,128)S(1)}, u32[]{:S(2)}, u32[]{:S(2)}) collective-permute-start(f32[16,72,128]{2,1,0:T(8,128)S(1)} %get-tuple-element.16), channel_id=1, source_target_pairs={{0,1},{1,0},{2,3},{3,2},{4,5},{5,4},{6,7},{7,6},{8,9},{9,8},{10,11... | collective-permute-start | bytes 1769480 | tf_op jit(solution)/shard_map/ppermute | solution.py:402
  10.2 1.6 %collective-permute-done = f32[16,72,128]{2,1,0:T(8,128)S(1)} collective-permute-done((f32[16,72,128]{2,1,0:T(8,128)S(1)}, f32[16,72,128]{2,1,0:T(8,128)S(1)}, u32[]{:S(2)}, u32[]{:S(2)}) %collective-permute-start) | collective-permute-done | bytes 589856 | tf_op jit(solution)/shard_map/ppermute | solution.py:402
  11.9 0.3 fusion
  12.2 19.0 %all_to_all.10 = f16[16,72,128]{2,1,0:T(8,128)(2,1)S(1)} all-to-all(f16[16,72,128]{2,1,0:T(8,128)(2,1)S(1)} %fusion), channel_id=1, replica_groups=mesh['group'=2,'chip'=8,'core'=2] {'group','chip'}, dimensions={0} | all-to-all | bytes 589824 | tf_op jit(solution)/shard_map/all_to_all | solution.py:403
  31.2 0.1 bitcast_add_fusion
  31.3 0.1 fusion.31
  31.5 13.2 %all_to_all.11.mine_ref = bf16[16,72,128]{2,1,0:T(8,128)(2,1)S(1)} all-to-all(bf16[16,72,128]{2,1,0:T(8,128)(2,1)S(1)} %broadcast_in_dim.13), channel_id=1, replica_groups=mesh['group'=2,'chip'=8,'core'=2] {'group','chip'}, dimensions={0} | all-to-all | bytes 589824 | tf_op jit(solution)/shard_map/all_to_all | solution.py:416
  44.7 0.0 collective-permute-start.1
  44.7 1.6 %collective-permute-done.1.other_ref = bf16[16,72,128]{2,1,0:T(8,128)(2,1)S(1)} collective-permute-done((bf16[16,72,128]{2,1,0:T(8,128)(2,1)S(1)}, bf16[16,72,128]{2,1,0:T(8,128)(2,1)S(1)}, u32[]{:S(2)}, u32[]{:S(2)}) %collective-permute-start.1) | collective-permute-done | bytes 294944 | tf_op jit(solution)/shard_map/ppermute | solution.py:417
  46.2 1.6 %finish.1 = (bf16[64,3072]{1,0:T(8,128)(2,1)}, bf16[64,1536]{1,0:T(8,128)(2,1)}, f32[64,144]{1,0:T(8,128)}, f32[64,144]{1,0:T(8,128)}) custom-call(s32[2]{0:T(128)S(1)} %pad_add_fusion.refs_0_.where_ref, bf16[16,72,128]{2,1,0:T(8,128)(2,1)S(1)} %all_to_all.11.mine_ref, bf16[16,72,128]{2,1,0:T(8,128)(2,1)S(1)} %collective-permute-done.1.other_ref, ...), custom_call_target="tpu_custom_call" | custom-call | tf_op jit(solution)/shard_map/finish/pallas_call | solution.py:328
  (3 shorter events, 0.1 us)
Async XLA Ops:
  9.7 2.1 %collective-permute-start = (f32[16,72,128]{2,1,0:T(8,128)S(1)}, f32[16,72,128]{2,1,0:T(8,128)S(1)}, u32[]{:S(2)}, u32[]{:S(2)}) collective-permute-start(f32[16,72,128]{2,1,0:T(8,128)S(1)} %get-tuple-element.16), channel_id=1, source_target_pairs={{0,1},{1,0},{2,3},{3,2},{4,5},{5,4},{6,7},{7,6},{8,9},{9,8},{10,11... | collective-permute-start | bytes 1769480 | tf_op jit(solution)/shard_map/ppermute | solution.py:402
  44.7 1.6 %collective-permute-start.1 = (bf16[16,72,128]{2,1,0:T(8,128)(2,1)S(1)}, bf16[16,72,128]{2,1,0:T(8,128)(2,1)S(1)}, u32[]{:S(2)}, u32[]{:S(2)}) collective-permute-start(bf16[16,72,128]{2,1,0:T(8,128)(2,1)S(1)} %all_to_all.11.mine_ref), channel_id=1, source_target_pairs={{0,1},{1,0},{2,3},{3,2},{4,5},{5,4},{6,7},{7,6},{8,9},{9,8},{10,11... | collective-permute-start | bytes 884744 | tf_op jit(solution)/shard_map/ppermute | solution.py:417

commit v6 on v5

--- a/solution.py
+++ b/solution.py
@@ -20,6 +20,7 @@
 LANES = 128
 SUB = 8
 RANGE = 2.0**-11
+TINY = 2.0**-100
 PIECES = 2
 F32 = jnp.float32
 BF16 = jnp.bfloat16
@@ -341,8 +342,8 @@
 
 
 def coded_of(g):
-    root = jnp.sqrt(jnp.abs(g) * RANGE)
-    return jnp.where(g < 0, -root, root).astype(jnp.float16)
+    g = g * RANGE
+    return (g * lax.rsqrt(jnp.maximum(jnp.abs(g), TINY))).astype(jnp.float16)
 
 
 def decoded_of(code):
@@ -399,7 +400,8 @@
         params = rows_of(lax.dynamic_slice_in_dim(combined, index * own, own, 1)).astype(F32)
         first, second = rows_of(first_moment.T), rows_of(second_moment.T)
 
-    coded = coded_of(keep + lax.ppermute(send, "core", SWAP))
+    other = decoded_of(lax.ppermute(coded_of(send), "core", SWAP)) / RANGE
+    coded = coded_of(keep + other)
     arrived = lax.all_to_all(coded, CHIPS, 0, 0, tiled=True)
     grads = None
     for k in range(chips):

time: 48 us -> 47.7 us (level)
  no operation moved by 1% of the time
where the time goes in v6:
time: 47.7 us; the launch traced here: 47.5 us
  blocking collectives  32.2 us (68%)
  Pallas kernels  10.6 us (22%)
  waiting for transfers between devices  2.78 us (6%)
  other arithmetic  0.69 us (1%)
  between operations  0.68 us (1%)
  starting transfers between devices  0.52 us (1%)
    all_to_all x1, blocking collectives, on_device(): arrived = lax.all_to_all(coded, CHIPS, 0, 0, tiled=True)  19 us
    all_to_all x1, blocking collectives, on_device(): mine = lax.all_to_all(copies, CHIPS, 0, 0, tiled=True)  13.2 us
    pallas_call x1, Pallas kernels, backward(): pl.pallas_call(functools.partial(backward_kernel, steps, packed=packed),...  9.01 us
    ppermute x1, waiting for transfers between devices, on_device(): other = lax.ppermute(mine, 'core', SWAP)  1.57 us
    pallas_call x1, Pallas kernels, finish(): pl.pallas_call(finish_kernel, in_specs=[pl.BlockSpec(memory_space=pltpu.S...  1.56 us
    ppermute x1, waiting for transfers between devices, on_device(): other = decoded_of(lax.ppermute(coded_of(send), 'core', SWAP)) / RANGE  1.21 us
  transfers between devices with their start and end apart: 2, of which 2 were waited for; matrix products, arithmetic and copies ran while one was open for 0% of the time, Pallas kernels for 0%

profile of v6, /device:TPU:0, one launch (start us, length us, event | category | flops | bytes accessed | tf_op | source)
XLA Modules:
  0.0 47.5 jit_solution(17925979496872936602)
XLA Ops:
  0.6 0.1 pad_add_fusion.refs_0_.where_ref
  0.7 9.0 %backward.1 = (f32[16,72,128]{2,1,0:T(8,128)S(1)}, f32[16,72,128]{2,1,0:T(8,128)S(1)}, f32[3,72,128]{2,1,0:T(8,128)S(1)}) custom-call(s32[2]{0:T(128)S(1)} %pad_add_fusion.refs_0_.where_ref, bf16[320,3072]{1,0:T(8,128)(2,1)} %refs_1_.1, bf16[3072,1536]{1,0:T(8,128)(2,1)} %refs_2_.1, f32[1,128]{1,0:T(1,128)} %bitcast.162, bf16[64,3072]{1,0:T(8,128)(2,1)} %bitcast.157, ...), custom_call_target="tpu_custom_call" | custom-call | tf_op jit(solution)/shard_map/backward/pallas_call | solution.py:314
  9.7 0.1 multiply_convert_fusion.1
  9.9 0.5 %collective-permute-start = (f16[16,72,128]{2,1,0:T(8,128)(2,1)S(1)}, f16[16,72,128]{2,1,0:T(8,128)(2,1)S(1)}, u32[]{:S(2)}, u32[]{:S(2)}) collective-permute-start(f16[16,72,128]{2,1,0:T(8,128)(2,1)S(1)} %multiply_convert_fusion.1), channel_id=1, source_target_pairs={{0,1},{1,0},{2,3},{3,2},{4,5},{5,4},{6,7},{7,6},{8,9},{9,8},{10,11... | collective-permute-start | bytes 884744 | tf_op jit(solution)/shard_map/ppermute | solution.py:403
  10.4 1.2 %collective-permute-done = f16[16,72,128]{2,1,0:T(8,128)(2,1)S(1)} collective-permute-done((f16[16,72,128]{2,1,0:T(8,128)(2,1)S(1)}, f16[16,72,128]{2,1,0:T(8,128)(2,1)S(1)}, u32[]{:S(2)}, u32[]{:S(2)}) %collective-permute-start) | collective-permute-done | bytes 294944 | tf_op jit(solution)/shard_map/ppermute | solution.py:403
  11.6 0.2 multiply_convert_fusion
  11.8 19.0 %all_to_all.10 = f16[16,72,128]{2,1,0:T(8,128)(2,1)S(1)} all-to-all(f16[16,72,128]{2,1,0:T(8,128)(2,1)S(1)} %multiply_convert_fusion), channel_id=1, replica_groups=mesh['group'=2,'chip'=8,'core'=2] {'group','chip'}, dimensions={0} | all-to-all | bytes 589824 | tf_op jit(solution)/shard_map/all_to_all | solution.py:405
  30.9 0.1 bitcast_add_fusion
  31.0 0.1 fusion.33
  31.1 13.2 %all_to_all.11.mine_ref = bf16[16,72,128]{2,1,0:T(8,128)(2,1)S(1)} all-to-all(bf16[16,72,128]{2,1,0:T(8,128)(2,1)S(1)} %broadcast_in_dim.13), channel_id=1, replica_groups=mesh['group'=2,'chip'=8,'core'=2] {'group','chip'}, dimensions={0} | all-to-all | bytes 589824 | tf_op jit(solution)/shard_map/all_to_all | solution.py:418
  44.3 0.0 collective-permute-start.1
  44.3 1.6 %collective-permute-done.1.other_ref = bf16[16,72,128]{2,1,0:T(8,128)(2,1)S(1)} collective-permute-done((bf16[16,72,128]{2,1,0:T(8,128)(2,1)S(1)}, bf16[16,72,128]{2,1,0:T(8,128)(2,1)S(1)}, u32[]{:S(2)}, u32[]{:S(2)}) %collective-permute-start.1) | collective-permute-done | bytes 294944 | tf_op jit(solution)/shard_map/ppermute | solution.py:419
  45.9 1.6 %finish.1 = (bf16[64,3072]{1,0:T(8,128)(2,1)}, bf16[64,1536]{1,0:T(8,128)(2,1)}, f32[64,144]{1,0:T(8,128)}, f32[64,144]{1,0:T(8,128)}) custom-call(s32[2]{0:T(128)S(1)} %pad_add_fusion.refs_0_.where_ref, bf16[16,72,128]{2,1,0:T(8,128)(2,1)S(1)} %all_to_all.11.mine_ref, bf16[16,72,128]{2,1,0:T(8,128)(2,1)S(1)} %collective-permute-done.1.other_ref, ...), custom_call_target="tpu_custom_call" | custom-call | tf_op jit(solution)/shard_map/finish/pallas_call | solution.py:329
  (3 shorter events, 0.1 us)
Async XLA Ops:
  9.9 1.7 %collective-permute-start = (f16[16,72,128]{2,1,0:T(8,128)(2,1)S(1)}, f16[16,72,128]{2,1,0:T(8,128)(2,1)S(1)}, u32[]{:S(2)}, u32[]{:S(2)}) collective-permute-start(f16[16,72,128]{2,1,0:T(8,128)(2,1)S(1)} %multiply_convert_fusion.1), channel_id=1, source_target_pairs={{0,1},{1,0},{2,3},{3,2},{4,5},{5,4},{6,7},{7,6},{8,9},{9,8},{10,11... | collective-permute-start | bytes 884744 | tf_op jit(solution)/shard_map/ppermute | solution.py:403
  44.3 1.6 %collective-permute-start.1 = (bf16[16,72,128]{2,1,0:T(8,128)(2,1)S(1)}, bf16[16,72,128]{2,1,0:T(8,128)(2,1)S(1)}, u32[]{:S(2)}, u32[]{:S(2)}) collective-permute-start(bf16[16,72,128]{2,1,0:T(8,128)(2,1)S(1)} %all_to_all.11.mine_ref), channel_id=1, source_target_pairs={{0,1},{1,0},{2,3},{3,2},{4,5},{5,4},{6,7},{7,6},{8,9},{9,8},{10,11... | collective-permute-start | bytes 884744 | tf_op jit(solution)/shard_map/ppermute | solution.py:419

commit v7 on v6

--- a/solution.py
+++ b/solution.py
@@ -58,13 +58,13 @@
 
 def backward_kernel(steps, *refs, packed):
     if packed:
-        (where_ref, hidden_h, w_h, gain_h, down_h, up_h, cot_h, first_h, second_h) = refs[:9]
-        (keep_ref, send_ref, own_ref) = refs[9:12]
-        (hidden, w, gain, down, up, cot, project_s, grad_s, back_s, turned, grads_s, first_s, second_s, sems) = refs[12:]
+        (hidden_h, w_h, gain_h, down_h, up_h, cot_h, first_h, second_h) = refs[:8]
+        (keep_ref, send_ref, own_ref) = refs[8:11]
+        (hidden, w, gain, down, up, cot, project_s, grad_s, back_s, turned, grads_s, first_s, second_s, sems) = refs[11:]
     else:
-        (where_ref, hidden_h, w_h, gain_h, down_h, up_h, cot_h) = refs[:7]
-        grads_s = refs[7]
-        (hidden, w, gain, down, up, cot, project_s, grad_s, back_s, turned, sems) = refs[8:]
+        (hidden_h, w_h, gain_h, down_h, up_h, cot_h) = refs[:6]
+        grads_s = refs[6]
+        (hidden, w, gain, down, up, cot, project_s, grad_s, back_s, turned, sems) = refs[7:]
     tokens, model_width = hidden_h.shape
     width = w.shape[2]
     head = gain.shape[1]
@@ -180,12 +180,12 @@
     if packed:
         for copy in single[3:]:
             copy.wait()
-        pack_blocks(where_ref, grads_s, down, up, first_s, second_s, keep_ref, send_ref, own_ref)
-
-
-def pack_blocks(where_ref, grads_s, down, up, first_s, second_s, keep_ref, send_ref, own_ref):
+        pack_blocks(grads_s, down, up, first_s, second_s, keep_ref, send_ref, own_ref)
+
+
+def pack_blocks(grads_s, down, up, first_s, second_s, keep_ref, send_ref, own_ref):
     lane = lanes_of((64, LANES))
-    core = where_ref[1]
+    core = lax.axis_index("core")
     on_zero = jnp.full((SUB, LANES), core, jnp.int32) == 0
     on_zero_main = jnp.full((64, LANES), core, jnp.int32) == 0
 
@@ -208,7 +208,7 @@
     for group in reversed(range(keep_ref.shape[0] // (SUB // 2))):
         pack_group(group)
 
-    index = where_ref[0]
+    index = lax.axis_index(EVERY)
     j = index % SUB
     tile = index // SUB * (SUB + 1) + j
     tiles = down.shape[1] // LANES
@@ -229,9 +229,9 @@
         own_ref[n, 64:72] = pack_tail(last, 0)
 
 
-def finish_kernel(where_ref, mine_ref, other_ref, own_ref, down_ref, up_ref, first_ref, second_ref):
+def finish_kernel(mine_ref, other_ref, own_ref, down_ref, up_ref, first_ref, second_ref):
     lane = lanes_of((64, LANES))
-    core = where_ref[1]
+    core = lax.axis_index("core")
     on_zero = jnp.full((72, LANES), core, jnp.int32) == 0
     down_tiles = down_ref.shape[1] // LANES
     blocks = {}
@@ -266,13 +266,13 @@
         else:
             up_ref[:, (tile - down_tiles) * LANES : (tile - down_tiles + 1) * LANES] = out
 
-    j = where_ref[0] % SUB
+    j = lax.axis_index(EVERY) % SUB
     for n, ref in ((0, first_ref), (1, second_ref)):
         ref[:, :LANES] = pltpu.roll(own_ref[n, :64], (LANES - 16 * j) % LANES, 1)
         ref[:, LANES:] = unpack_tail(own_ref[n, 64:72], 0)[:, :16]
 
 
-def backward(where, hidden, w_query, gain, down_t, up, cotangent, first_t, second_t, chips, packed):
+def backward(hidden, w_query, gain, down_t, up, cotangent, first_t, second_t, chips, packed):
     tokens, model_width = hidden.shape
     features = w_query.shape[1]
     rank = down_t.shape[0]
@@ -313,22 +313,22 @@
     operands = [pltpu.with_memory_space_constraint(x, pltpu.HBM) for x in operands]
     return pl.pallas_call(
         functools.partial(backward_kernel, steps, packed=packed),
-        in_specs=[pl.BlockSpec(memory_space=pltpu.SMEM)] + [far] * len(operands),
+        in_specs=[far] * len(operands),
         out_specs=out_specs,
         out_shape=out_shape,
         scratch_shapes=scratch,
         compiler_params=pltpu.CompilerParams(vmem_limit_bytes=32 << 20),
         name="backward",
-    )(where, *operands)
-
-
-def finish(where, mine, other, own_new, model_width, features):
+    )(*operands)
+
+
+def finish(mine, other, own_new, model_width, features):
     rank = 64
     own = own_new.shape[1] * LANES // rank
     full = pl.BlockSpec(memory_space=pltpu.VMEM)
     return pl.pallas_call(
         finish_kernel,
-        in_specs=[pl.BlockSpec(memory_space=pltpu.SMEM), full, full, full],
+        in_specs=[full, full, full],
         out_specs=[full] * 4,
         out_shape=[
             jax.ShapeDtypeStruct((rank, model_width), BF16),
@@ -338,7 +338,7 @@
         ],
         compiler_params=pltpu.CompilerParams(vmem_limit_bytes=32 << 20),
         name="finish",
-    )(where, mine, other, own_new)
+    )(mine, other, own_new)
 
 
 def coded_of(g):
@@ -374,10 +374,8 @@
     packed = rank == 64 and own == LANES + 16 and model_width % LANES == 0 and chips % 4 == 0
     core = lax.axis_index("core")
     index = lax.axis_index(EVERY)
-    where = jnp.stack([index, core]).astype(jnp.int32)
     down_t = down_projection_matrix.T
     result = backward(
-        where,
         hidden_in,
         w_query,
         query_gain[None, :],
@@ -419,7 +417,7 @@
     other = lax.ppermute(mine, "core", SWAP)
     if packed:
         own_new = jnp.stack([first_new, second_new])
-        down_new, up_new, first_out, second_out = finish(where, mine, other, own_new, model_width, features)
+        down_new, up_new, first_out, second_out = finish(mine, other, own_new, model_width, features)
     else:
         pair = jnp.stack([mine, other])
         pair = jnp.where(core == 0, pair, pair[::-1])

time: 47.7 us -> 46.6 us (0.977)
  Pallas kernels: 10.6 us -> 9.51 us
    pallas_call x1, Pallas kernels: 1.56 us -> 1.02 us  [finish(): pl.pallas_call(finish_kernel, in_specs=[full, full, full], out_specs=[ful...]
    pallas_call x1, Pallas kernels: 9.01 us -> 8.48 us  [backward(): pl.pallas_call(functools.partial(backward_kernel, steps, packed=packed),...]
where the time goes in v7:
time: 46.6 us; the launch traced here: 46.3 us
  blocking collectives  32.2 us (69%)
  Pallas kernels  9.51 us (20%)
  waiting for transfers between devices  2.78 us (6%)
  between operations  0.67 us (1%)
  other arithmetic  0.62 us (1%)
  starting transfers between devices  0.51 us (1%)
    all_to_all x1, blocking collectives, on_device(): arrived = lax.all_to_all(coded, CHIPS, 0, 0, tiled=True)  19 us
    all_to_all x1, blocking collectives, on_device(): mine = lax.all_to_all(copies, CHIPS, 0, 0, tiled=True)  13.2 us
    pallas_call x1, Pallas kernels, backward(): pl.pallas_call(functools.partial(backward_kernel, steps, packed=packed),...  8.48 us
    ppermute x1, waiting for transfers between devices, on_device(): other = lax.ppermute(mine, 'core', SWAP)  1.57 us
    ppermute x1, waiting for transfers between devices, on_device(): other = decoded_of(lax.ppermute(coded_of(send), 'core', SWAP)) / RANGE  1.21 us
    pallas_call x1, Pallas kernels, finish(): pl.pallas_call(finish_kernel, in_specs=[full, full, full], out_specs=[ful...  1.02 us
  transfers between devices with their start and end apart: 2, of which 2 were waited for; matrix products, arithmetic and copies ran while one was open for 0% of the time, Pallas kernels for 0%

profile of v7, /device:TPU:0, one launch (start us, length us, event | category | flops | bytes accessed | tf_op | source)
XLA Modules:
  0.0 46.3 jit_solution(10236227668649504550)
XLA Ops:
  0.6 8.5 %backward.1 = (f32[16,72,128]{2,1,0:T(8,128)S(1)}, f32[16,72,128]{2,1,0:T(8,128)S(1)}, f32[3,72,128]{2,1,0:T(8,128)S(1)}) custom-call(bf16[320,3072]{1,0:T(8,128)(2,1)} %refs_0_.1, bf16[3072,1536]{1,0:T(8,128)(2,1)} %refs_1_.1, f32[1,128]{1,0:T(1,128)} %bitcast.160, bf16[64,3072]{1,0:T(8,128)(2,1)} %bitcast.155, bf16[64,1536]{1,0:T(8,128)(2,1)} %refs_4_.1, ...), custom_call_target="tpu_custom_call" | custom-call | tf_op jit(solution)/shard_map/backward/pallas_call | solution.py:314
  9.1 0.1 multiply_convert_fusion.1
  9.3 0.5 %collective-permute-start = (f16[16,72,128]{2,1,0:T(8,128)(2,1)S(1)}, f16[16,72,128]{2,1,0:T(8,128)(2,1)S(1)}, u32[]{:S(2)}, u32[]{:S(2)}) collective-permute-start(f16[16,72,128]{2,1,0:T(8,128)(2,1)S(1)} %multiply_convert_fusion.1), channel_id=1, source_target_pairs={{0,1},{1,0},{2,3},{3,2},{4,5},{5,4},{6,7},{7,6},{8,9},{9,8},{10,11... | collective-permute-start | bytes 884744 | tf_op jit(solution)/shard_map/ppermute | solution.py:401
  9.8 1.2 %collective-permute-done = f16[16,72,128]{2,1,0:T(8,128)(2,1)S(1)} collective-permute-done((f16[16,72,128]{2,1,0:T(8,128)(2,1)S(1)}, f16[16,72,128]{2,1,0:T(8,128)(2,1)S(1)}, u32[]{:S(2)}, u32[]{:S(2)}) %collective-permute-start) | collective-permute-done | bytes 294944 | tf_op jit(solution)/shard_map/ppermute | solution.py:401
  11.0 0.2 multiply_convert_fusion
  11.2 19.0 %all_to_all.10 = f16[16,72,128]{2,1,0:T(8,128)(2,1)S(1)} all-to-all(f16[16,72,128]{2,1,0:T(8,128)(2,1)S(1)} %multiply_convert_fusion), channel_id=1, replica_groups=mesh['group'=2,'chip'=8,'core'=2] {'group','chip'}, dimensions={0} | all-to-all | bytes 589824 | tf_op jit(solution)/shard_map/all_to_all | solution.py:403
  30.3 0.1 bitcast_add_fusion
  30.4 0.1 fusion.33
  30.6 13.2 %all_to_all.11.mine_ref = bf16[16,72,128]{2,1,0:T(8,128)(2,1)S(1)} all-to-all(bf16[16,72,128]{2,1,0:T(8,128)(2,1)S(1)} %broadcast_in_dim.13), channel_id=1, replica_groups=mesh['group'=2,'chip'=8,'core'=2] {'group','chip'}, dimensions={0} | all-to-all | bytes 589824 | tf_op jit(solution)/shard_map/all_to_all | solution.py:416
  43.7 0.0 collective-permute-start.1
  43.7 1.6 %collective-permute-done.1.other_ref = bf16[16,72,128]{2,1,0:T(8,128)(2,1)S(1)} collective-permute-done((bf16[16,72,128]{2,1,0:T(8,128)(2,1)S(1)}, bf16[16,72,128]{2,1,0:T(8,128)(2,1)S(1)}, u32[]{:S(2)}, u32[]{:S(2)}) %collective-permute-start.1) | collective-permute-done | bytes 294944 | tf_op jit(solution)/shard_map/ppermute | solution.py:417
  45.3 1.0 %finish.1 = (bf16[64,3072]{1,0:T(8,128)(2,1)}, bf16[64,1536]{1,0:T(8,128)(2,1)}, f32[64,144]{1,0:T(8,128)}, f32[64,144]{1,0:T(8,128)}) custom-call(bf16[16,72,128]{2,1,0:T(8,128)(2,1)S(1)} %all_to_all.11.mine_ref, bf16[16,72,128]{2,1,0:T(8,128)(2,1)S(1)} %collective-permute-done.1.other_ref, f32[2,72,128]{2,1,0:T(8,128)S(1)} %pad_maximum_fusion.own_ref), custom_call_target="tpu_custom_call" | custom-call | tf_op jit(solution)/shard_map/finish/pallas_call | solution.py:329
  (3 shorter events, 0.1 us)
Async XLA Ops:
  9.3 1.7 %collective-permute-start = (f16[16,72,128]{2,1,0:T(8,128)(2,1)S(1)}, f16[16,72,128]{2,1,0:T(8,128)(2,1)S(1)}, u32[]{:S(2)}, u32[]{:S(2)}) collective-permute-start(f16[16,72,128]{2,1,0:T(8,128)(2,1)S(1)} %multiply_convert_fusion.1), channel_id=1, source_target_pairs={{0,1},{1,0},{2,3},{3,2},{4,5},{5,4},{6,7},{7,6},{8,9},{9,8},{10,11... | collective-permute-start | bytes 884744 | tf_op jit(solution)/shard_map/ppermute | solution.py:401
  43.7 1.6 %collective-permute-start.1 = (bf16[16,72,128]{2,1,0:T(8,128)(2,1)S(1)}, bf16[16,72,128]{2,1,0:T(8,128)(2,1)S(1)}, u32[]{:S(2)}, u32[]{:S(2)}) collective-permute-start(bf16[16,72,128]{2,1,0:T(8,128)(2,1)S(1)} %all_to_all.11.mine_ref), channel_id=1, source_target_pairs={{0,1},{1,0},{2,3},{3,2},{4,5},{5,4},{6,7},{7,6},{8,9},{9,8},{10,11... | collective-permute-start | bytes 884744 | tf_op jit(solution)/shard_map/ppermute | solution.py:417

commit v8 on v7

--- a/solution.py
+++ b/solution.py
@@ -59,8 +59,8 @@
 def backward_kernel(steps, *refs, packed):
     if packed:
         (hidden_h, w_h, gain_h, down_h, up_h, cot_h, first_h, second_h) = refs[:8]
-        (keep_ref, send_ref, own_ref) = refs[8:11]
-        (hidden, w, gain, down, up, cot, project_s, grad_s, back_s, turned, grads_s, first_s, second_s, sems) = refs[11:]
+        (both_ref, own_ref) = refs[8:10]
+        (hidden, w, gain, down, up, cot, project_s, grad_s, back_s, turned, grads_s, first_s, second_s, sems) = refs[10:]
     else:
         (hidden_h, w_h, gain_h, down_h, up_h, cot_h) = refs[:6]
         grads_s = refs[6]
@@ -180,14 +180,11 @@
     if packed:
         for copy in single[3:]:
             copy.wait()
-        pack_blocks(grads_s, down, up, first_s, second_s, keep_ref, send_ref, own_ref)
-
-
-def pack_blocks(grads_s, down, up, first_s, second_s, keep_ref, send_ref, own_ref):
+        pack_blocks(grads_s, down, up, first_s, second_s, both_ref, own_ref)
+
+
+def pack_blocks(grads_s, down, up, first_s, second_s, both_ref, own_ref):
     lane = lanes_of((64, LANES))
-    core = lax.axis_index("core")
-    on_zero = jnp.full((SUB, LANES), core, jnp.int32) == 0
-    on_zero_main = jnp.full((64, LANES), core, jnp.int32) == 0
 
     def tile_of(t):
         return grads_s[:, t * LANES : (t + 1) * LANES]
@@ -199,13 +196,13 @@
 
     def pack_group(group):
         for k in range(SUB // 2):
-            even, odd = block_of(group, 2 * k), block_of(group, 2 * k + 1)
             chip = group * (SUB // 2) + k
-            for ref, (one, two) in ((keep_ref, (even, odd)), (send_ref, (odd, even))):
-                ref[chip, :64] = jnp.where(on_zero_main, one[0], two[0])
-                ref[chip, 64:72] = jnp.where(on_zero, one[1], two[1])
-
-    for group in reversed(range(keep_ref.shape[0] // (SUB // 2))):
+            for core in range(2):
+                main, tail = block_of(group, 2 * k + core)
+                both_ref[core, chip, :64] = main
+                both_ref[core, chip, 64:72] = tail
+
+    for group in reversed(range(both_ref.shape[1] // (SUB // 2))):
         pack_group(group)
 
     index = lax.axis_index(EVERY)
@@ -299,12 +296,13 @@
     if packed:
         own = rows // chips // 2
         height = rank * own // LANES
-        halves = (chips, height, LANES)
+        halves = (2, chips, height, LANES)
         operands += [first_t, second_t]
-        out_shape = [jax.ShapeDtypeStruct(halves, F32)] * 2 + [
-            jax.ShapeDtypeStruct((3, height, LANES), F32)
+        out_shape = [
+            jax.ShapeDtypeStruct(halves, F32),
+            jax.ShapeDtypeStruct((3, height, LANES), F32),
         ]
-        out_specs = [near] * 3
+        out_specs = [near] * 2
         scratch += [pltpu.VMEM((rank, rows), F32)] + [pltpu.VMEM((rank, own), F32)] * 2
     else:
         out_shape = jax.ShapeDtypeStruct((rank, rows), F32)
@@ -388,16 +386,16 @@
         packed,
     )
     if packed:
-        keep, send, own_state = result
+        blocks, own_state = result
         params, first, second = own_state[0], own_state[1], own_state[2]
     else:
         blocks = result.reshape(rank, chips, 2, own).transpose(2, 1, 0, 3).reshape(2, chips, -1, LANES)
-        keep = lax.dynamic_index_in_dim(blocks, core, 0, keepdims=False)
-        send = lax.dynamic_index_in_dim(blocks, 1 - core, 0, keepdims=False)
         combined = jnp.concatenate([down_t, up_projection_matrix], axis=1)
         params = rows_of(lax.dynamic_slice_in_dim(combined, index * own, own, 1)).astype(F32)
         first, second = rows_of(first_moment.T), rows_of(second_moment.T)
 
+    keep = lax.dynamic_index_in_dim(blocks, core, 0, keepdims=False)
+    send = lax.dynamic_index_in_dim(blocks, 1 - core, 0, keepdims=False)
     other = decoded_of(lax.ppermute(coded_of(send), "core", SWAP)) / RANGE
     coded = coded_of(keep + other)
     arrived = lax.all_to_all(coded, CHIPS, 0, 0, tiled=True)

time: 46.6 us -> 46.6 us (level)
  no operation moved by 1% of the time
where the time goes in v8:
time: 46.6 us; the launch traced here: 46.3 us
  blocking collectives  32.2 us (69%)
  Pallas kernels  9.5 us (20%)
  waiting for transfers between devices  2.78 us (6%)
  between operations  0.68 us (1%)
  other arithmetic  0.63 us (1%)
  starting transfers between devices  0.52 us (1%)
    all_to_all x1, blocking collectives, on_device(): arrived = lax.all_to_all(coded, CHIPS, 0, 0, tiled=True)  19 us
    all_to_all x1, blocking collectives, on_device(): mine = lax.all_to_all(copies, CHIPS, 0, 0, tiled=True)  13.2 us
    pallas_call x1, Pallas kernels, backward(): pl.pallas_call(functools.partial(backward_kernel, steps, packed=packed),...  8.47 us
    ppermute x1, waiting for transfers between devices, on_device(): other = lax.ppermute(mine, 'core', SWAP)  1.57 us
    ppermute x1, waiting for transfers between devices, on_device(): other = decoded_of(lax.ppermute(coded_of(send), 'core', SWAP)) / RANGE  1.21 us
    pallas_call x1, Pallas kernels, finish(): pl.pallas_call(finish_kernel, in_specs=[full, full, full], out_specs=[ful...  1.02 us
  transfers between devices with their start and end apart: 2, of which 2 were waited for; matrix products, arithmetic and copies ran while one was open for 0% of the time, Pallas kernels for 0%

profile of v8, /device:TPU:0, one launch (start us, length us, event | category | flops | bytes accessed | tf_op | source)
XLA Modules:
  0.0 46.3 jit_solution(6957438457808716299)
XLA Ops:
  0.6 8.5 %backward.1 = (f32[2,16,72,128]{3,2,1,0:T(8,128)S(1)}, f32[3,72,128]{2,1,0:T(8,128)S(1)}) custom-call(bf16[320,3072]{1,0:T(8,128)(2,1)} %refs_0_.1, bf16[3072,1536]{1,0:T(8,128)(2,1)} %refs_1_.1, f32[1,128]{1,0:T(1,128)} %bitcast.175, bf16[64,3072]{1,0:T(8,128)(2,1)} %bitcast.170, bf16[64,1536]{1,0:T(8,128)(2,1)} %refs_4_.1, bf16[320,1536]{1,0:T(8,128)(2,1)} %refs_5_.1, ...), custom_call_target="tpu_custom_call" | custom-call | tf_op jit(solution)/shard_map/backward/pallas_call | solution.py:312
  9.1 0.2 fusion.5
  9.3 0.5 %collective-permute-start = (f16[16,72,128]{2,1,0:T(8,128)(2,1)S(1)}, f16[16,72,128]{2,1,0:T(8,128)(2,1)S(1)}, u32[]{:S(2)}, u32[]{:S(2)}) collective-permute-start(f16[16,72,128]{2,1,0:T(8,128)(2,1)S(1)} %fusion.5), channel_id=1, source_target_pairs={{0,1},{1,0},{2,3},{3,2},{4,5},{5,4},{6,7},{7,6},{8,9},{9,8},{10,11... | collective-permute-start | bytes 884744 | tf_op jit(solution)/shard_map/ppermute | solution.py:399
  9.8 1.2 %collective-permute-done = f16[16,72,128]{2,1,0:T(8,128)(2,1)S(1)} collective-permute-done((f16[16,72,128]{2,1,0:T(8,128)(2,1)S(1)}, f16[16,72,128]{2,1,0:T(8,128)(2,1)S(1)}, u32[]{:S(2)}, u32[]{:S(2)}) %collective-permute-start) | collective-permute-done | bytes 294944 | tf_op jit(solution)/shard_map/ppermute | solution.py:399
  11.0 0.2 multiply_convert_fusion
  11.3 19.0 %all_to_all.10 = f16[16,72,128]{2,1,0:T(8,128)(2,1)S(1)} all-to-all(f16[16,72,128]{2,1,0:T(8,128)(2,1)S(1)} %multiply_convert_fusion), channel_id=1, replica_groups=mesh['group'=2,'chip'=8,'core'=2] {'group','chip'}, dimensions={0} | all-to-all | bytes 589824 | tf_op jit(solution)/shard_map/all_to_all | solution.py:401
  30.3 0.1 bitcast_add_fusion
  30.4 0.1 fusion.36
  30.6 13.2 %all_to_all.11.mine_ref = bf16[16,72,128]{2,1,0:T(8,128)(2,1)S(1)} all-to-all(bf16[16,72,128]{2,1,0:T(8,128)(2,1)S(1)} %broadcast_in_dim.13), channel_id=1, replica_groups=mesh['group'=2,'chip'=8,'core'=2] {'group','chip'}, dimensions={0} | all-to-all | bytes 589824 | tf_op jit(solution)/shard_map/all_to_all | solution.py:414
  43.7 0.0 collective-permute-start.1
  43.7 1.6 %collective-permute-done.1.other_ref = bf16[16,72,128]{2,1,0:T(8,128)(2,1)S(1)} collective-permute-done((bf16[16,72,128]{2,1,0:T(8,128)(2,1)S(1)}, bf16[16,72,128]{2,1,0:T(8,128)(2,1)S(1)}, u32[]{:S(2)}, u32[]{:S(2)}) %collective-permute-start.1) | collective-permute-done | bytes 294944 | tf_op jit(solution)/shard_map/ppermute | solution.py:415
  45.3 1.0 %finish.1 = (bf16[64,3072]{1,0:T(8,128)(2,1)}, bf16[64,1536]{1,0:T(8,128)(2,1)}, f32[64,144]{1,0:T(8,128)}, f32[64,144]{1,0:T(8,128)}) custom-call(bf16[16,72,128]{2,1,0:T(8,128)(2,1)S(1)} %all_to_all.11.mine_ref, bf16[16,72,128]{2,1,0:T(8,128)(2,1)S(1)} %collective-permute-done.1.other_ref, f32[2,72,128]{2,1,0:T(8,128)S(1)} %pad_maximum_fusion.own_ref), custom_call_target="tpu_custom_call" | custom-call | tf_op jit(solution)/shard_map/finish/pallas_call | solution.py:327
  (3 shorter events, 0.1 us)
Async XLA Ops:
  9.3 1.7 %collective-permute-start = (f16[16,72,128]{2,1,0:T(8,128)(2,1)S(1)}, f16[16,72,128]{2,1,0:T(8,128)(2,1)S(1)}, u32[]{:S(2)}, u32[]{:S(2)}) collective-permute-start(f16[16,72,128]{2,1,0:T(8,128)(2,1)S(1)} %fusion.5), channel_id=1, source_target_pairs={{0,1},{1,0},{2,3},{3,2},{4,5},{5,4},{6,7},{7,6},{8,9},{9,8},{10,11... | collective-permute-start | bytes 884744 | tf_op jit(solution)/shard_map/ppermute | solution.py:399
  43.7 1.6 %collective-permute-start.1 = (bf16[16,72,128]{2,1,0:T(8,128)(2,1)S(1)}, bf16[16,72,128]{2,1,0:T(8,128)(2,1)S(1)}, u32[]{:S(2)}, u32[]{:S(2)}) collective-permute-start(bf16[16,72,128]{2,1,0:T(8,128)(2,1)S(1)} %all_to_all.11.mine_ref), channel_id=1, source_target_pairs={{0,1},{1,0},{2,3},{3,2},{4,5},{5,4},{6,7},{7,6},{8,9},{9,8},{10,11... | collective-permute-start | bytes 884744 | tf_op jit(solution)/shard_map/ppermute | solution.py:415
